TPU v7x, 32 devices: a whole 2x2x4 slice. The times are simulated.
32 devices in a mesh: clips: 2 (over x), gx: 4 (over y, core), gy: 4 (over z).
Axes of the slice: x: 2, y: 2, z: 4, core: 2. Of those that a mesh axis runs over, the one named last changes fastest.
Arguments:
- fields: float32 [12, 32, 32, 512], P('clips', None, 'gx', 'gy'), parts along dimension 0, may hold values from -6 to 6
- material_map: int32 [64, 32, 512], P('clips', 'gx', 'gy'), parts along dimension 0, may hold values from 0 to 3
- material_eps: float32 [4], replicated, may hold values from 1 to 4
- material_loss: float32 [4], replicated, may hold values from 0 to 0.4
- source_shift: int32 [64, 2], P(('gx', 'gy')), may hold values from -8 to 8
- source_mask: int32 [64, 96, 96], P(('gx', 'gy')), may hold values 0 or 1
- source_weight: float32 [64], P(('gx', 'gy')), may hold values from 0.25 to 4
Outputs:
- final_fields: float32 [12, 32, 32, 512], P('clips', None, 'gx', 'gy'), parts along dimension 0
- image: float32 [512, 1024], P(('gx', 'gy'), 'clips'), parts along dimension 1
There are 2 independent parts, one for each index of `clips`. A program takes and returns all parts, laid end to end along the dimension named above; an argument that names none is the same for every part. Nothing has to cross between parts.
All inputs are finite; a program needn't handle non-finite values. No bound on the sum of `source_mask` on one device may be relied on, other than what follows from the above.
Results may differ from a plain program's by a relative error of at most 0.0014.
The roundings to bfloat16 on the way count: a program that leaves them out, or rounds other values in their place, can miss the bound.
Values sent between devices are 32-bit elements; how exact they have to be, the bound alone decides.
A program may use at most 64 MiB of HBM per device.

v0:
```python
import math

import jax
import jax.numpy as jnp
from jax import lax
from jax.sharding import PartitionSpec as P

STEPS = 12
M = 512


COURANT = 0.55
ANGULAR = 0.7
PRECISE = lax.Precision.HIGHEST


def padded_2(cells, sides, width):
    for axis, dim in sides:
        count = lax.axis_size(axis)
        ends = count - 1
        head = lax.slice_in_dim(cells, 0, width, axis=dim)
        tail = lax.slice_in_dim(cells, cells.shape[dim] - width, cells.shape[dim], axis=dim)
        cells = jnp.concatenate(
            [
                lax.ppermute(tail, axis, [(i, (i + 1) % count) for i in range(ends)]),
                cells,
                lax.ppermute(head, axis, [((i + 1) % count, i) for i in range(ends)]),
            ],
            axis=dim,
        )
    return cells


def ahead(values, dimension, border):
    remainder = lax.slice_in_dim(values, 1, values.shape[dimension], axis=dimension)
    return jnp.concatenate((remainder, border), dimension)


def behind(values, dimension, border):
    remainder = lax.slice_in_dim(values, 0, values.shape[dimension] - 1, axis=dimension)
    return jnp.concatenate((border, remainder), dimension)


def blank(values, dimension):
    extent = list(values.shape)
    extent[dimension] = 1
    return jnp.zeros(extent, values.dtype)


def magnetic(efield, hfield, borders):

    def change(component, dimension):
        border = borders.get((component, dimension))
        border = blank(efield[component], dimension)
        return ahead(efield[component], dimension, border) - efield[component]

    new_x = hfield[0] - COURANT * (change(2, 2) - change(1, 0))
    new_y = hfield[1] - COURANT * (change(0, 0) - change(2, 1))
    new_z = hfield[2] - COURANT * (change(1, 1) - change(0, 2))
    return (new_x, new_y, new_z)


def electric(efield, hfield, coef_keep, coef_curl, borders):

    def change(component, dimension):
        border = borders.get((component, dimension))
        border = blank(hfield[component], dimension)
        return hfield[component] - behind(hfield[component], dimension, border)

    new_x = coef_keep * efield[0] + coef_curl * (change(2, 2) - change(1, 0))
    new_y = coef_keep * efield[1] + coef_curl * (change(0, 0) - change(2, 1))
    new_z = coef_keep * efield[2] + coef_curl * (change(1, 1) - change(0, 2))
    return (new_x, new_y, new_z)


def lookup(materials, values_table):
    running = jnp.zeros(materials.shape, jnp.float32)
    for material in range(values_table.shape[0]):
        running = running + jnp.where(materials == material, values_table[material], 0.0)
    return running


def spectrum(extent, orders, offset, period):
    cell_ids = jnp.arange(extent, dtype=jnp.int32) + offset
    order_ids = jnp.arange(orders, dtype=jnp.int32) - orders // 2
    wrapped = order_ids[:, None] * cell_ids[None, :] % period
    angles = 2.0 * math.pi / period * wrapped.astype(jnp.float32)
    return (jnp.cos(angles), jnp.sin(angles))


def image_tables(pixels, orders_p, orders_q):
    cos_u, sin_u = spectrum(pixels, orders_p, 0, pixels)
    row_table = (jnp.concatenate((cos_u.T, sin_u.T), 1) * (1.0 / math.sqrt(orders_p))).astype(
        jnp.bfloat16
    )
    cos_v, sin_v = spectrum(pixels, orders_q, 0, pixels)
    real_v = (cos_v * (1.0 / math.sqrt(orders_q))).astype(jnp.bfloat16)
    imag_v = (sin_v * (1.0 / math.sqrt(orders_q))).astype(jnp.bfloat16)
    g_matrix = jnp.concatenate(
        (jnp.concatenate((real_v, imag_v), 1), jnp.concatenate((-imag_v, real_v), 1)), 0
    )
    return (row_table, g_matrix)


def source_columns(masked, g_matrix, pixels):
    halves = jnp.concatenate(
        (
            jnp.concatenate((masked[0, 0], masked[1, 0]), 1),
            jnp.concatenate((masked[0, 1], masked[1, 1]), 1),
        ),
        0,
    )
    spread = jnp.dot(halves, g_matrix, preferred_element_type=jnp.float32).astype(jnp.bfloat16)
    count_p = masked.shape[2]
    real_x = spread[:count_p, :pixels]
    imag_x = spread[:count_p, pixels:]
    real_y = spread[count_p:, :pixels]
    imag_y = spread[count_p:, pixels:]
    upper = jnp.concatenate((real_x, imag_x, real_y, imag_y), 1)
    lower = jnp.concatenate((-imag_x, real_x, -imag_y, real_y), 1)
    return jnp.concatenate((upper, lower), 0)


def project(cos_x, sin_x, part_re, part_im):
    order_re = jnp.einsum("px,cxq->cpq", cos_x, part_re, precision=PRECISE) + jnp.einsum(
        "px,cxq->cpq", sin_x, part_im, precision=PRECISE
    )
    order_im = jnp.einsum("px,cxq->cpq", cos_x, part_im, precision=PRECISE) - jnp.einsum(
        "px,cxq->cpq", sin_x, part_re, precision=PRECISE
    )
    return (order_re, order_im)


def body(
    fields, material_map, material_eps, material_loss, source_shift, source_mask, source_weight
):
    tiles_x = lax.axis_size("gx")
    tiles_y = lax.axis_size("gy")
    depth, cells_x, cells_y = (fields.shape[1], fields.shape[2], fields.shape[3])
    middle = depth // 2
    keep_table = (1.0 - material_loss) / (1.0 + material_loss)
    curl_table = COURANT / (material_eps * (1.0 + material_loss))
    efield = (fields[0], fields[1], fields[2])
    hfield = (fields[3], fields[4], fields[5])
    zeros_plane = jnp.zeros((2, cells_x, cells_y), jnp.float32)
    materials = padded_2(material_map, (("gx", 1), ("gy", 2)), 3)
    coef_keep = lookup(materials, keep_table)
    coef_curl = lookup(materials, curl_table)
    global_x = lax.axis_index("gx") * cells_x - 3 + jnp.arange(cells_x + 6, dtype=jnp.int32)
    global_y = lax.axis_index("gy") * cells_y - 3 + jnp.arange(cells_y + 6, dtype=jnp.int32)
    rows_in = (global_x >= 0) & (global_x < cells_x * tiles_x)
    cols_in = (global_y >= 0) & (global_y < cells_y * tiles_y)
    inside = (rows_in[:, None] & cols_in[None, :]).astype(jnp.float32)

    def advance_block(turn_index, state_now):
        efield, hfield, phase_re, phase_im = state_now
        padded = padded_2(jnp.stack(efield + hfield), (("gx", 2), ("gy", 3)), 3)
        e_wide = (padded[0], padded[1], padded[2])
        h_wide = (padded[3], padded[4], padded[5])
        for substep in range(3):
            h_wide = tuple((values * inside for values in magnetic(e_wide, h_wide, {})))
            e_wide = tuple(
                (values * inside for values in electric(e_wide, h_wide, coef_keep, coef_curl, {}))
            )
            moment = jnp.float32(ANGULAR) * (3 * turn_index + substep + 1).astype(jnp.float32)
            monitor = jnp.stack((e_wide[0][middle, 3:-3, 3:-3], e_wide[1][middle, 3:-3, 3:-3]))
            phase_re = phase_re + monitor * jnp.cos(moment)
            phase_im = phase_im - monitor * jnp.sin(moment)
        efield = tuple((values[:, 3:-3, 3:-3] for values in e_wide))
        hfield = tuple((values[:, 3:-3, 3:-3] for values in h_wide))
        return (efield, hfield, phase_re, phase_im)

    efield, hfield, phase_re, phase_im = lax.fori_loop(
        0, STEPS // 3, advance_block, (efield, hfield, zeros_plane, zeros_plane)
    )
    final_fields = jnp.stack(efield + hfield)
    orders_p = source_mask.shape[1]
    orders_q = source_mask.shape[2]
    period_x = cells_x * tiles_x
    period_y = cells_y * tiles_y
    cos_x, sin_x = spectrum(cells_x, orders_p, lax.axis_index("gx") * cells_x, period_x)
    cos_y, sin_y = spectrum(cells_y, orders_q, lax.axis_index("gy") * cells_y, period_y)
    part_re = jnp.einsum("cxy,qy->cxq", phase_re, cos_y, precision=PRECISE) + jnp.einsum(
        "cxy,qy->cxq", phase_im, sin_y, precision=PRECISE
    )
    part_im = jnp.einsum("cxy,qy->cxq", phase_im, cos_y, precision=PRECISE) - jnp.einsum(
        "cxy,qy->cxq", phase_re, sin_y, precision=PRECISE
    )
    order_re, order_im = project(cos_x, sin_x, part_re, part_im)
    order_re, order_im = lax.psum((order_re, order_im), ("gx", "gy"))
    scaling = 1.0 / math.sqrt(period_x * period_y * STEPS)
    orders_b = (jnp.stack((order_re, order_im)) * scaling).astype(jnp.bfloat16)
    pixels = M
    row_table, g_matrix = image_tables(pixels, orders_p, orders_q)
    ids_p = jnp.arange(orders_p, dtype=jnp.int32)
    ids_q = jnp.arange(orders_q, dtype=jnp.int32)

    def prepare(inputs):
        offsets, passed = inputs
        pick_x = (ids_p[None, :] == (ids_p[:, None] + offsets[0]) % orders_p).astype(jnp.bfloat16)
        pick_y = (ids_q[None, :] == (ids_q[:, None] + offsets[1]) % orders_q).astype(jnp.bfloat16)
        rolled = jnp.einsum(
            "pa,kcab->kcpb", pick_x, orders_b, preferred_element_type=jnp.float32
        ).astype(jnp.bfloat16)
        rolled = jnp.einsum(
            "kcpb,qb->kcpq", rolled, pick_y, preferred_element_type=jnp.float32
        ).astype(jnp.bfloat16)
        masked = rolled * passed.astype(jnp.bfloat16)
        return source_columns(masked, g_matrix, pixels)

    columns_all = lax.map(prepare, (source_shift, source_mask))
    sources_all = source_weight.shape[0] * tiles_x * tiles_y
    strip_rows = pixels // (tiles_x * tiles_y)

    def add_source(source_at, running):
        fields_img = jnp.dot(row_table, columns_all[source_at], preferred_element_type=jnp.float32)
        squared = fields_img * fields_img
        bright = squared.reshape(strip_rows * lax.axis_size(("gx", "gy")), 4, pixels).sum(axis=1)
        return running + source_weight[source_at] / sources_all * bright

    image = lax.psum_scatter(
        lax.fori_loop(
            0,
            columns_all.shape[0],
            add_source,
            jnp.zeros((strip_rows * lax.axis_size(("gx", "gy")), pixels), jnp.float32),
        ),
        ("gx", "gy"),
        scatter_dimension=0,
        tiled=True,
    )
    return (final_fields, image)


def solution(mesh):
    placed = (
        P("clips", None, "gx", "gy"),
        P("clips", "gx", "gy"),
        P(),
        P(),
        P(("gx", "gy"), None),
        P(("gx", "gy"), None, None),
        P(("gx", "gy")),
    )
    return jax.shard_map(
        body,
        mesh=mesh,
        in_specs=placed,
        out_specs=(P("clips", None, "gx", "gy"), P(("gx", "gy"), "clips")),
        check_vma=False,
    )
```

profile of v0, /device:TPU:0, one launch (start us, length us, event | category | flops | bytes accessed | tf_op | source)
XLA Modules:
  0.0 467.1 jit_solution(8237598422946285970)
XLA Ops:
  21.8 4.3 collective-permute-start.6
  27.5 3.1 collective-permute-done.6
  30.5 4.7 %collective-permute-done.7 = s32[32,14,3]{2,0,1:T(8,128)S(1)} collective-permute-done((s32[32,14,3]{2,0,1:T(8,128)S(1)}, s32[32,14,3]{2,0,1:T(8,128)S(1)}, u32[]{:S(2)}, u32[]{:S(2)}) %collective-permute-start.7) | collective-permute-done | bytes 5408 | tf_op jit(solution)/shard_map/ppermute | solution.py:27
  35.3 3.7 select_add_fusion.2
  39.0 3.4 select_add_fusion.3
  42.4 208.5 %while.60 = (s32[]{:T(128)}, f32[32,8,128]{2,0,1:T(8,128)}, f32[32,8,128]{2,0,1:T(8,128)}, f32[32,8,128]{2,0,1:T(8,128)}, f32[32,8,128]{2,0,1:T(8,128)}, /*index...) while((s32[]{:T(128)}, f32[32,8,128]{2,0,1:T(8,128)}, ...), condition=%wide.region_1.2_spmd.clone, body=%wide.region_0.1_spmd.clone.sunk | while | flops 8286133 | bytes 65248444 | solution.py:173
  51.4 4.3 collective-permute-start.1
  61.6 3.3 pad_maximum_fusion.7
  69.0 4.6 collective-permute-start.3
  74.1 5.5 %copy.168 = f32[6,32,14,128]{3,1,2,0:T(8,128)} copy(f32[6,32,14,128]{1,2,3,0:T(8,128)} %copy-done) | data formatting | bytes 2752512 | tf_op jit(solution)/shard_map/while/body/eval_jaxpr/concatenate | solution.py:23
  102.9 4.2 collective-permute-start.1
  113.1 3.3 pad_maximum_fusion.7
  120.4 4.6 collective-permute-start.3
  125.6 5.5 %copy.168 = f32[6,32,14,128]{3,1,2,0:T(8,128)} copy(f32[6,32,14,128]{1,2,3,0:T(8,128)} %copy-done) | data formatting | bytes 2752512 | tf_op jit(solution)/shard_map/while/body/eval_jaxpr/concatenate | solution.py:23
  154.4 5.3 %collective-permute-start.1 = (f32[6,32,3,128]{3,1,2,0:T(8,128)}, f32[6,32,3,128]{3,1,2,0:T(8,128)}, u32[]{:S(2)}, u32[]{:S(2)}) collective-permute-start(f32[6,32,3,128]{3,1,2,0:T(8,128)} %copy.165), channel_id=1, source_target_pairs={{0,4},{4,8},{8,12},{1,5},{5,9},{9,13},{2,6},{6,10},{10,14},{3,7},{... | collective-permute-start | bytes 884744 | tf_op jit(solution)/shard_map/while/body/eval_jaxpr/ppermute | solution.py:25
  165.7 3.3 pad_maximum_fusion.7
  173.1 4.6 collective-permute-start.3
  178.3 5.5 %copy.168 = f32[6,32,14,128]{3,1,2,0:T(8,128)} copy(f32[6,32,14,128]{1,2,3,0:T(8,128)} %copy-done) | data formatting | bytes 2752512 | tf_op jit(solution)/shard_map/while/body/eval_jaxpr/concatenate | solution.py:23
  207.1 5.3 %collective-permute-start.1 = (f32[6,32,3,128]{3,1,2,0:T(8,128)}, f32[6,32,3,128]{3,1,2,0:T(8,128)}, u32[]{:S(2)}, u32[]{:S(2)}) collective-permute-start(f32[6,32,3,128]{3,1,2,0:T(8,128)} %copy.165), channel_id=1, source_target_pairs={{0,4},{4,8},{8,12},{1,5},{5,9},{9,13},{2,6},{6,10},{10,14},{3,7},{... | collective-permute-start | bytes 884744 | tf_op jit(solution)/shard_map/while/body/eval_jaxpr/ppermute | solution.py:25
  218.4 3.3 pad_maximum_fusion.7
  225.7 4.6 collective-permute-start.3
  230.9 5.5 %copy.168 = f32[6,32,14,128]{3,1,2,0:T(8,128)} copy(f32[6,32,14,128]{1,2,3,0:T(8,128)} %copy-done) | data formatting | bytes 2752512 | tf_op jit(solution)/shard_map/while/body/eval_jaxpr/concatenate | solution.py:23
  256.8 92.4 %all-reduce.39.cloned.1.call-done = (f32[1,2,96,96]{2,3,1,0:T(8,128)}, f32[1,2,96,96]{2,3,1,0:T(8,128)}) async-done(((f32[1,2,96,96]{2,3,1,0:T(8,128)}, f32[1,2,96,96]{2,3,1,0:T(8,128)}), (f32[1,2,96,96]{2,3,1,0:T(8,128)}, f32[1,2,96,96]{2,3,1,0:T(8,128)})) %all-reduce.39.cloned.1.call-update) | async-done | bytes 147472 | tf_op jit(solution)/shard_map/psum | solution.py:190
  350.4 18.7 %while.59 = (s32[]{:T(128)}, bf16[4,192,2048]{2,1,0:T(8,128)(2,1)}, s32[4,2]{0,1:T(2,128)S(1)}, bf16[2,2,96,96]{3,2,1,0:T(8,128)(2,1)S(1)}, s32[4,96,96]{2,1,0:T...) while((s32[]{:T(128)}, bf16[4,192,2048]{2,1,0:T(8,128)(2,1)}, ...), condition=%wide.region_5.6_spmd.clone.clone, body=%wide.region_4.5_spmd.clone.clone.sunk | while | flops 95211840 | bytes 4524157 | solution.py:211
  369.1 33.2 %while.61 = (s32[]{:T(128)}, f32[512,512]{0,1:T(8,128)S(1)}, f32[4]{0:T(128)S(1)}, bf16[4,192,2048]{2,1,0:T(8,128)(2,1)}, bf16[512,192]{1,0:T(8,128)(2,1)S(1)}, ...) while((s32[]{:T(128)}, f32[512,512]{0,1:T(8,128)S(1)}, f32[4]{0:T(128)S(1)}, ...), condition=%wide.region_8.9_spmd.clone, body=%wide.region_6.8_spmd.clone.sunk | while | flops 405274624 | bytes 13566599 | solution.py:222
  369.1 3.9 convolution_multiply_fusion.2
  373.0 2.8 reduce_sum.15
  377.4 3.9 convolution_multiply_fusion.2
  381.3 2.8 reduce_sum.15
  385.7 3.9 convolution_multiply_fusion.2
  394.0 3.9 convolution_multiply_fusion.2
  409.6 50.6 %reduce-scatter.2.cloned.1.call-done = f32[32,512]{1,0:T(8,128)} async-done(((f32[512,512]{1,0:T(8,128)}), f32[32,512]{1,0:T(8,128)}) %reduce-scatter.2.cloned.1.call-update) | async-done | bytes 65552 | tf_op jit(solution)/shard_map/reduce_scatter | solution.py:221
  (431 shorter events, 189.9 us)
Async XLA Ops:
  7.2 14.4 %copy-start.6 = (s32[32,8,128]{2,1,0:T(8,128)S(1)}, s32[32,8,128]{2,1,0:T(8,128)}, u32[]{:S(2)}) copy-start(s32[32,8,128]{2,1,0:T(8,128)} %param.14) | copy-start | bytes 393220
  7.2 10.1 %copy-start.13 = (f32[4]{0:T(128)S(1)}, f32[4]{0:T(128)}, u32[]{:S(2)}) copy-start(f32[4]{0:T(128)} %param.15) | copy-start | bytes 52
  7.2 342.1 %all-reduce.39.cloned.1.call-start = ((), (), s32[]{:S(2)}) async-start(), calls=%async_computation.2 | async-start | bytes 393216 | tf_op jit(solution)/shard_map/psum | solution.py:190
  8.3 13.3 %collective-permute-start.4 = (s32[32,3,128]{2,0,1:T(8,128)S(1)}, s32[32,3,128]{2,0,1:T(8,128)S(1)}, u32[]{:S(2)}, u32[]{:S(2)}) collective-permute-start(s32[32,3,128]{2,0,1:T(8,128)S(1)} %copy.138), channel_id=1, source_target_pairs={{0,4},{4,8},{8,12},{1,5},{5,9},{9,13},{2,6},{6,10},{10,14},{3,7},{... | collective-permute-start | bytes 147464 | tf_op jit(solution)/shard_map/ppermute | solution.py:25
  10.7 11.0 %collective-permute-start.5 = (s32[32,3,128]{2,0,1:T(8,128)S(1)}, s32[32,3,128]{2,0,1:T(8,128)S(1)}, u32[]{:S(2)}, u32[]{:S(2)}) collective-permute-start(s32[32,3,128]{2,0,1:T(8,128)S(1)} %copy.139), channel_id=1, source_target_pairs={{4,0},{8,4},{12,8},{5,1},{9,5},{13,9},{6,2},{10,6},{14,10},{7,3},{... | collective-permute-start | bytes 147464 | tf_op jit(solution)/shard_map/ppermute | solution.py:27
  21.8 8.8 %collective-permute-start.6 = (s32[32,14,3]{2,0,1:T(8,128)S(1)}, s32[32,14,3]{2,0,1:T(8,128)S(1)}, u32[]{:S(2)}, u32[]{:S(2)}) collective-permute-start(s32[32,14,3]{2,0,1:T(8,128)S(1)} %get-tuple-element.745), channel_id=1, source_target_pairs={{0,1},{1,2},{2,3},{4,5},{5,6},{6,7},{8,9},{9,10},{10,11},{12,13},{... | collective-permute-start | bytes 16136 | tf_op jit(solution)/shard_map/ppermute | solution.py:25
  26.1 9.2 %collective-permute-start.7 = (s32[32,14,3]{2,0,1:T(8,128)S(1)}, s32[32,14,3]{2,0,1:T(8,128)S(1)}, u32[]{:S(2)}, u32[]{:S(2)}) collective-permute-start(s32[32,14,3]{2,0,1:T(8,128)S(1)} %get-tuple-element.746), channel_id=1, source_target_pairs={{1,0},{2,1},{3,2},{5,4},{6,5},{7,6},{9,8},{10,9},{11,10},{13,12},{... | collective-permute-start | bytes 16136 | tf_op jit(solution)/shard_map/ppermute | solution.py:27
  42.4 208.6 %copy-start.9 = (s32[96]{0:T(128)S(1)}, s32[96]{0:T(128)}, u32[]{:S(2)}) copy-start(s32[96]{0:T(128)} %copy-done.8) | copy-start | bytes 1156
  42.4 208.6 %copy-start.15 = (s32[128]{0:T(128)S(1)}, s32[128]{0:T(128)}, u32[]{:S(2)}) copy-start(s32[128]{0:T(128)} %iota_add_fusion.3) | copy-start | bytes 1540
  42.4 210.3 %copy-start.11 = (s32[8]{0:T(128)S(1)}, s32[8]{0:T(128)}, u32[]{:S(2)}) copy-start(s32[8]{0:T(128)} %iota_add_fusion.2) | copy-start | bytes 100
  49.3 8.4 %collective-permute-start = (f32[6,32,3,128]{3,1,2,0:T(8,128)}, f32[6,32,3,128]{3,1,2,0:T(8,128)S(1)}, u32[]{:S(2)}, u32[]{:S(2)}) collective-permute-start(f32[6,32,3,128]{3,1,2,0:T(8,128)} %copy.162), channel_id=1, source_target_pairs={{4,0},{8,4},{12,8},{5,1},{9,5},{13,9},{6,2},{10,6},{14,10},{7,3},{... | collective-permute-start | bytes 884744 | tf_op jit(solution)/shard_map/while/body/eval_jaxpr/ppermute | solution.py:27
  51.4 7.9 %collective-permute-start.1 = (f32[6,32,3,128]{3,1,2,0:T(8,128)}, f32[6,32,3,128]{3,1,2,0:T(8,128)}, u32[]{:S(2)}, u32[]{:S(2)}) collective-permute-start(f32[6,32,3,128]{3,1,2,0:T(8,128)} %copy.165), channel_id=1, source_target_pairs={{0,4},{4,8},{8,12},{1,5},{5,9},{9,13},{2,6},{6,10},{10,14},{3,7},{... | collective-permute-start | bytes 884744 | tf_op jit(solution)/shard_map/while/body/eval_jaxpr/ppermute | solution.py:25
  67.7 12.0 %collective-permute-start.2 = (f32[6,32,14,3]{1,2,3,0:T(8,128)S(1)}, f32[6,32,14,3]{1,2,3,0:T(8,128)S(1)}, u32[]{:S(2)}, u32[]{:S(2)}) collective-permute-start(f32[6,32,14,3]{1,2,3,0:T(8,128)S(1)} %get-tuple-element.974), channel_id=1, source_target_pairs={{1,0},{2,1},{3,2},{5,4},{6,5},{7,6},{9,8},{10,9},{11,10},{13,12},{... | collective-permute-start | bytes 96776 | tf_op jit(solution)/shard_map/while/body/eval_jaxpr/ppermute | solution.py:27
  69.0 11.3 %collective-permute-start.3 = (f32[6,32,14,3]{1,2,3,0:T(8,128)S(1)}, f32[6,32,14,3]{1,2,3,0:T(8,128)S(1)}, u32[]{:S(2)}, u32[]{:S(2)}) collective-permute-start(f32[6,32,14,3]{1,2,3,0:T(8,128)S(1)} %get-tuple-element.975), channel_id=1, source_target_pairs={{0,1},{1,2},{2,3},{4,5},{5,6},{6,7},{8,9},{9,10},{10,11},{12,13},{... | collective-permute-start | bytes 96776 | tf_op jit(solution)/shard_map/while/body/eval_jaxpr/ppermute | solution.py:25
  100.9 8.4 %collective-permute-start = (f32[6,32,3,128]{3,1,2,0:T(8,128)}, f32[6,32,3,128]{3,1,2,0:T(8,128)S(1)}, u32[]{:S(2)}, u32[]{:S(2)}) collective-permute-start(f32[6,32,3,128]{3,1,2,0:T(8,128)} %copy.162), channel_id=1, source_target_pairs={{4,0},{8,4},{12,8},{5,1},{9,5},{13,9},{6,2},{10,6},{14,10},{7,3},{... | collective-permute-start | bytes 884744 | tf_op jit(solution)/shard_map/while/body/eval_jaxpr/ppermute | solution.py:27
  102.9 7.8 %collective-permute-start.1 = (f32[6,32,3,128]{3,1,2,0:T(8,128)}, f32[6,32,3,128]{3,1,2,0:T(8,128)}, u32[]{:S(2)}, u32[]{:S(2)}) collective-permute-start(f32[6,32,3,128]{3,1,2,0:T(8,128)} %copy.165), channel_id=1, source_target_pairs={{0,4},{4,8},{8,12},{1,5},{5,9},{9,13},{2,6},{6,10},{10,14},{3,7},{... | collective-permute-start | bytes 884744 | tf_op jit(solution)/shard_map/while/body/eval_jaxpr/ppermute | solution.py:25
  119.1 12.0 %collective-permute-start.2 = (f32[6,32,14,3]{1,2,3,0:T(8,128)S(1)}, f32[6,32,14,3]{1,2,3,0:T(8,128)S(1)}, u32[]{:S(2)}, u32[]{:S(2)}) collective-permute-start(f32[6,32,14,3]{1,2,3,0:T(8,128)S(1)} %get-tuple-element.974), channel_id=1, source_target_pairs={{1,0},{2,1},{3,2},{5,4},{6,5},{7,6},{9,8},{10,9},{11,10},{13,12},{... | collective-permute-start | bytes 96776 | tf_op jit(solution)/shard_map/while/body/eval_jaxpr/ppermute | solution.py:27
  120.4 11.3 %collective-permute-start.3 = (f32[6,32,14,3]{1,2,3,0:T(8,128)S(1)}, f32[6,32,14,3]{1,2,3,0:T(8,128)S(1)}, u32[]{:S(2)}, u32[]{:S(2)}) collective-permute-start(f32[6,32,14,3]{1,2,3,0:T(8,128)S(1)} %get-tuple-element.975), channel_id=1, source_target_pairs={{0,1},{1,2},{2,3},{4,5},{5,6},{6,7},{8,9},{9,10},{10,11},{12,13},{... | collective-permute-start | bytes 96776 | tf_op jit(solution)/shard_map/while/body/eval_jaxpr/ppermute | solution.py:25
  152.4 9.5 %collective-permute-start = (f32[6,32,3,128]{3,1,2,0:T(8,128)}, f32[6,32,3,128]{3,1,2,0:T(8,128)S(1)}, u32[]{:S(2)}, u32[]{:S(2)}) collective-permute-start(f32[6,32,3,128]{3,1,2,0:T(8,128)} %copy.162), channel_id=1, source_target_pairs={{4,0},{8,4},{12,8},{5,1},{9,5},{13,9},{6,2},{10,6},{14,10},{7,3},{... | collective-permute-start | bytes 884744 | tf_op jit(solution)/shard_map/while/body/eval_jaxpr/ppermute | solution.py:27
  154.4 9.0 %collective-permute-start.1 = (f32[6,32,3,128]{3,1,2,0:T(8,128)}, f32[6,32,3,128]{3,1,2,0:T(8,128)}, u32[]{:S(2)}, u32[]{:S(2)}) collective-permute-start(f32[6,32,3,128]{3,1,2,0:T(8,128)} %copy.165), channel_id=1, source_target_pairs={{0,4},{4,8},{8,12},{1,5},{5,9},{9,13},{2,6},{6,10},{10,14},{3,7},{... | collective-permute-start | bytes 884744 | tf_op jit(solution)/shard_map/while/body/eval_jaxpr/ppermute | solution.py:25
  171.8 12.0 %collective-permute-start.2 = (f32[6,32,14,3]{1,2,3,0:T(8,128)S(1)}, f32[6,32,14,3]{1,2,3,0:T(8,128)S(1)}, u32[]{:S(2)}, u32[]{:S(2)}) collective-permute-start(f32[6,32,14,3]{1,2,3,0:T(8,128)S(1)} %get-tuple-element.974), channel_id=1, source_target_pairs={{1,0},{2,1},{3,2},{5,4},{6,5},{7,6},{9,8},{10,9},{11,10},{13,12},{... | collective-permute-start | bytes 96776 | tf_op jit(solution)/shard_map/while/body/eval_jaxpr/ppermute | solution.py:27
  173.1 11.3 %collective-permute-start.3 = (f32[6,32,14,3]{1,2,3,0:T(8,128)S(1)}, f32[6,32,14,3]{1,2,3,0:T(8,128)S(1)}, u32[]{:S(2)}, u32[]{:S(2)}) collective-permute-start(f32[6,32,14,3]{1,2,3,0:T(8,128)S(1)} %get-tuple-element.975), channel_id=1, source_target_pairs={{0,1},{1,2},{2,3},{4,5},{5,6},{6,7},{8,9},{9,10},{10,11},{12,13},{... | collective-permute-start | bytes 96776 | tf_op jit(solution)/shard_map/while/body/eval_jaxpr/ppermute | solution.py:25
  205.0 9.5 %collective-permute-start = (f32[6,32,3,128]{3,1,2,0:T(8,128)}, f32[6,32,3,128]{3,1,2,0:T(8,128)S(1)}, u32[]{:S(2)}, u32[]{:S(2)}) collective-permute-start(f32[6,32,3,128]{3,1,2,0:T(8,128)} %copy.162), channel_id=1, source_target_pairs={{4,0},{8,4},{12,8},{5,1},{9,5},{13,9},{6,2},{10,6},{14,10},{7,3},{... | collective-permute-start | bytes 884744 | tf_op jit(solution)/shard_map/while/body/eval_jaxpr/ppermute | solution.py:27
  207.1 9.0 %collective-permute-start.1 = (f32[6,32,3,128]{3,1,2,0:T(8,128)}, f32[6,32,3,128]{3,1,2,0:T(8,128)}, u32[]{:S(2)}, u32[]{:S(2)}) collective-permute-start(f32[6,32,3,128]{3,1,2,0:T(8,128)} %copy.165), channel_id=1, source_target_pairs={{0,4},{4,8},{8,12},{1,5},{5,9},{9,13},{2,6},{6,10},{10,14},{3,7},{... | collective-permute-start | bytes 884744 | tf_op jit(solution)/shard_map/while/body/eval_jaxpr/ppermute | solution.py:25
  224.4 12.0 %collective-permute-start.2 = (f32[6,32,14,3]{1,2,3,0:T(8,128)S(1)}, f32[6,32,14,3]{1,2,3,0:T(8,128)S(1)}, u32[]{:S(2)}, u32[]{:S(2)}) collective-permute-start(f32[6,32,14,3]{1,2,3,0:T(8,128)S(1)} %get-tuple-element.974), channel_id=1, source_target_pairs={{1,0},{2,1},{3,2},{5,4},{6,5},{7,6},{9,8},{10,9},{11,10},{13,12},{... | collective-permute-start | bytes 96776 | tf_op jit(solution)/shard_map/while/body/eval_jaxpr/ppermute | solution.py:27
  225.7 11.3 %collective-permute-start.3 = (f32[6,32,14,3]{1,2,3,0:T(8,128)S(1)}, f32[6,32,14,3]{1,2,3,0:T(8,128)S(1)}, u32[]{:S(2)}, u32[]{:S(2)}) collective-permute-start(f32[6,32,14,3]{1,2,3,0:T(8,128)S(1)} %get-tuple-element.975), channel_id=1, source_target_pairs={{0,1},{1,2},{2,3},{4,5},{5,6},{6,7},{8,9},{9,10},{10,11},{12,13},{... | collective-permute-start | bytes 96776 | tf_op jit(solution)/shard_map/while/body/eval_jaxpr/ppermute | solution.py:25
  250.9 99.4 %copy-start.5 = (bf16[192,1024]{1,0:T(8,128)(2,1)S(1)}, bf16[192,1024]{1,0:T(8,128)(2,1)}, u32[]{:S(2)}) copy-start(bf16[192,1024]{1,0:T(8,128)(2,1)} %maximum_maximum_fusion) | copy-start | bytes 1179652
  251.0 99.4 %copy-start.7 = (s32[4,2]{0,1:T(2,128)S(1)}, s32[4,2]{0,1:T(2,128)}, u32[]{:S(2)}) copy-start(s32[4,2]{0,1:T(2,128)} %param.17) | copy-start | bytes 100
  255.5 204.7 %reduce-scatter.2.cloned.1.call-start = ((), (), s32[]{:S(2)}) async-start(), calls=%async_computation.1 | async-start | bytes 1114112 | tf_op jit(solution)/shard_map/reduce_scatter | solution.py:221
  350.4 18.7 %copy-start.4 = (f32[512,512]{0,1:T(8,128)S(1)}, f32[512,512]{0,1:T(8,128)}, u32[]{:S(2)}) copy-start(f32[512,512]{0,1:T(8,128)} %custom-call.2) | copy-start | bytes 3145732
  350.4 18.7 %copy-start.14 = (f32[4]{0:T(128)S(1)}, f32[4]{0:T(128)}, u32[]{:S(2)}) copy-start(f32[4]{0:T(128)} %param.19) | copy-start | bytes 52
  409.6 50.6 %copy-start.10 = (f32[6,32,8,128]{3,2,1,0:T(8,128)}, f32[6,32,8,128]{3,2,1,0:T(8,128)S(1)}, u32[]{:S(2)}) copy-start(f32[6,32,8,128]{3,2,1,0:T(8,128)S(1)} %bitcast_dynamic-update-slice_fusion.6) | copy-start | bytes 2359300
  (18 other events, 43.4 us)
Sparse Core Ops, SparseCore 0:
  255.7 93.5 all-reduce.38
  403.8 56.3 reduce-scatter.1
where the time goes:
time: 470 us; the launch traced here: 467 us
  waiting for transfers between devices  151 us (32%)
  local copies, waits for them, and re-layouts  133 us (28%)
  other arithmetic  81.8 us (17%)
  starting transfers between devices  56.9 us (12%)
  matrix products  23.1 us (5%)
  between operations  14.4 us (3%)
  loops' own time  6.56 us (1%)
    psum x1, waiting for transfers between devices, body(): order_re, order_im = lax.psum((order_re, order_im), ('gx', 'gy'))  92.4 us
    reduce_scatter x1, waiting for transfers between devices, body(): lax.psum_scatter(lax.fori_loop(0, columns_all.shape[0], add_source, jnp.z...  50.6 us
    ppermute x10, starting transfers between devices, padded_2(): lax.ppermute(tail, axis, [(i, (i + 1) % count) for i in range(ends)])  44 us
    while x60, local copies, waits for them, and re-layouts  38.5 us
    concatenate x8, other arithmetic, padded_2(): jnp.concatenate([lax.ppermute(tail, axis, [(i, (i + 1) % count) for i in...  23.2 us
    concatenate x5, local copies, waits for them, and re-layouts, padded_2(): jnp.concatenate([lax.ppermute(tail, axis, [(i, (i + 1) % count) for i in...  22.2 us
    dot_general x4, matrix products, add_source(): jnp.dot(row_table, columns_all[source_at], preferred_element_type=jnp.flo...  15.6 us
    mul x16, other arithmetic, advance_block(): values * inside  13.9 us
  transfers between devices with their start and end apart: 22, of which 4 were waited for; matrix products, arithmetic and copies ran while one was open for 13% of the time, Pallas kernels for 0%

commit v1 on v0

v1 whole, which is shorter than its diff:
```python
import functools
import math

import jax
import jax.numpy as jnp
import numpy as np
from jax import lax
from jax.experimental import pallas as pl
from jax.experimental.pallas import tpu as pltpu
from jax.sharding import PartitionSpec as P

STEPS = 12
M = 512
COURANT = 0.55
ANGULAR = 0.7
PRECISE = lax.Precision.HIGHEST
MESH = pl.DeviceIdType.MESH


def peer_at(index, tiles_y):
    return {"gx": index // tiles_y, "gy": lax.rem(index, tiles_y)}


def greet(me, count, tiles_y):
    barrier = pltpu.get_barrier_semaphore()

    def signal(k, unused):
        pl.semaphore_signal(
            barrier,
            inc=1,
            device_id=peer_at(lax.rem(me + k, count), tiles_y),
            device_id_type=MESH,
        )
        return unused

    lax.fori_loop(1, count, signal, 0)
    pl.semaphore_wait(barrier, count - 1)


def march(
    tiles_x,
    tiles_y,
    fields_ref,
    material_ref,
    eps_ref,
    loss_ref,
    wave_ref,
    final_ref,
    phasor_ref,
    e_ref,
    h_ref,
    keep_ref,
    curl_ref,
    row_out,
    row_e,
    row_h,
    col_out,
    col_e,
    col_h,
    phase,
    gathered,
    send_sem,
    recv_sem,
    gather_send,
    gather_recv,
):
    count = tiles_x * tiles_y
    depth, cells_x, cells_y = fields_ref.shape[1:]
    middle = depth // 2
    at_x = lax.axis_index("gx")
    at_y = lax.axis_index("gy")
    me = at_x * tiles_y + at_y
    tile = (cells_x, cells_y)
    row_id = lax.broadcasted_iota(jnp.int32, tile, 0)
    col_id = lax.broadcasted_iota(jnp.int32, tile, 1)
    last_row = row_id == cells_x - 1
    first_row = row_id == 0
    last_col = col_id == cells_y - 1
    first_col = col_id == 0
    blank = jnp.zeros(tile, jnp.float32)

    has_right_x = at_x < tiles_x - 1
    has_left_x = at_x > 0
    has_right_y = at_y < tiles_y - 1
    has_left_y = at_y > 0
    routes = (
        (row_out.at[0], row_e, {"gx": at_x - 1}, has_left_x, has_right_x),
        (col_out.at[0], col_e, {"gy": at_y - 1}, has_left_y, has_right_y),
        (row_out.at[1], row_h, {"gx": at_x + 1}, has_right_x, has_left_x),
        (col_out.at[1], col_h, {"gy": at_y + 1}, has_right_y, has_left_y),
    )

    def copy_of(slot):
        source, target, device, _, _ = routes[slot]
        return pltpu.make_async_remote_copy(
            src_ref=source,
            dst_ref=target,
            send_sem=send_sem.at[slot],
            recv_sem=recv_sem.at[slot],
            device_id=device,
            device_id_type=MESH,
        )

    def send(slot):
        @pl.when(routes[slot][3])
        def _():
            copy_of(slot).start()

    def sent(slot):
        @pl.when(routes[slot][3])
        def _():
            copy_of(slot).wait_send()

    def arrived(slot):
        @pl.when(routes[slot][4])
        def _():
            copy_of(slot).wait_recv()

    for halo in (row_e, row_h, col_e, col_h):
        halo[...] = jnp.zeros(halo.shape, jnp.float32)
    greet(me, count, tiles_y)

    keep_values = []
    curl_values = []
    for material in range(eps_ref.shape[0]):
        loss = jnp.full(tile, loss_ref[material], jnp.float32)
        eps = jnp.full(tile, eps_ref[material], jnp.float32)
        keep_values.append((1.0 - loss) / (1.0 + loss))
        curl_values.append(COURANT / (eps * (1.0 + loss)))
    for component in range(3):
        e_ref[component, depth] = blank
        h_ref[component, 0] = blank
    phase[...] = jnp.zeros(phase.shape, jnp.float32)

    def pack_columns(packed, z, first, second, column):
        packed = jnp.where(
            col_id == z, jnp.broadcast_to(first[:, column : column + 1], tile), packed
        )
        return jnp.where(
            col_id == depth + z,
            jnp.broadcast_to(second[:, column : column + 1], tile),
            packed,
        )

    def load(z, packed):
        materials = material_ref[z]
        keep = keep_values[0]
        curl = curl_values[0]
        for material in range(1, len(keep_values)):
            keep = jnp.where(materials == material, keep_values[material], keep)
            curl = jnp.where(materials == material, curl_values[material], curl)
        keep_ref[z] = keep
        curl_ref[z] = curl
        for component in range(3):
            e_ref[component, z] = fields_ref[component, z]
            h_ref[component, z + 1] = fields_ref[3 + component, z]
        row_out[0, 0, pl.ds(z, 1), :] = fields_ref[2, z][0:1]
        row_out[0, 1, pl.ds(z, 1), :] = fields_ref[1, z][0:1]
        return pack_columns(packed, z, fields_ref[2, z], fields_ref[0, z], 0)

    col_out[0] = lax.fori_loop(0, depth, load, blank, unroll=True)
    send(0)
    send(1)

    def step(turn, unused):
        arrived(0)
        arrived(1)
        edge = col_e[...]

        @pl.when(turn > 0)
        def _():
            sent(2)
            sent(3)

        def magnetic(z, packed):
            ex, ey, ez = e_ref[0, z], e_ref[1, z], e_ref[2, z]
            ex_up, ey_up = e_ref[0, z + 1], e_ref[1, z + 1]
            row_z = jnp.broadcast_to(row_e[0, pl.ds(z, 1), :], tile)
            row_y = jnp.broadcast_to(row_e[1, pl.ds(z, 1), :], tile)
            col_z = pltpu.roll(edge, cells_y - 1 - z, 1)
            col_x = pltpu.roll(edge, cells_y - 1 - depth - z, 1)
            dx_ez = jnp.where(last_row, row_z, pltpu.roll(ez, cells_x - 1, 0)) - ez
            dx_ey = jnp.where(last_row, row_y, pltpu.roll(ey, cells_x - 1, 0)) - ey
            dy_ez = jnp.where(last_col, col_z, pltpu.roll(ez, cells_y - 1, 1)) - ez
            dy_ex = jnp.where(last_col, col_x, pltpu.roll(ex, cells_y - 1, 1)) - ex
            hx = h_ref[0, z + 1] - COURANT * (dy_ez - (ey_up - ey))
            hy = h_ref[1, z + 1] - COURANT * ((ex_up - ex) - dx_ez)
            hz = h_ref[2, z + 1] - COURANT * (dx_ey - dy_ex)
            h_ref[0, z + 1] = hx
            h_ref[1, z + 1] = hy
            h_ref[2, z + 1] = hz
            row_out[1, 0, pl.ds(z, 1), :] = hz[cells_x - 1 : cells_x]
            row_out[1, 1, pl.ds(z, 1), :] = hy[cells_x - 1 : cells_x]
            return pack_columns(packed, z, hz, hx, cells_y - 1)

        col_out[1] = lax.fori_loop(0, depth, magnetic, blank, unroll=True)
        send(2)
        send(3)
        sent(0)
        sent(1)
        arrived(2)
        arrived(3)
        edge = col_h[...]

        def electric(z, packed):
            hx, hy, hz = h_ref[0, z + 1], h_ref[1, z + 1], h_ref[2, z + 1]
            hx_down, hy_down = h_ref[0, z], h_ref[1, z]
            row_z = jnp.broadcast_to(row_h[0, pl.ds(z, 1), :], tile)
            row_y = jnp.broadcast_to(row_h[1, pl.ds(z, 1), :], tile)
            col_z = pltpu.roll(edge, lax.rem(cells_y - z, cells_y), 1)
            col_x = pltpu.roll(edge, cells_y - depth - z, 1)
            dx_hz = hz - jnp.where(first_row, row_z, pltpu.roll(hz, 1, 0))
            dx_hy = hy - jnp.where(first_row, row_y, pltpu.roll(hy, 1, 0))
            dy_hz = hz - jnp.where(first_col, col_z, pltpu.roll(hz, 1, 1))
            dy_hx = hx - jnp.where(first_col, col_x, pltpu.roll(hx, 1, 1))
            keep, curl = keep_ref[z], curl_ref[z]
            ex = keep * e_ref[0, z] + curl * (dy_hz - (hy - hy_down))
            ey = keep * e_ref[1, z] + curl * ((hx - hx_down) - dx_hz)
            ez = keep * e_ref[2, z] + curl * (dx_hy - dy_hx)
            e_ref[0, z] = ex
            e_ref[1, z] = ey
            e_ref[2, z] = ez
            row_out[0, 0, pl.ds(z, 1), :] = ez[0:1]
            row_out[0, 1, pl.ds(z, 1), :] = ey[0:1]
            return pack_columns(packed, z, ez, ex, 0)

        col_out[0] = lax.fori_loop(0, depth, electric, blank, unroll=True)

        @pl.when(turn < STEPS - 1)
        def _():
            send(0)
            send(1)

        for component in range(2):
            monitor = e_ref[component, middle]
            phase[component] = phase[component] + monitor * wave_ref[0, turn]
            phase[2 + component] = phase[2 + component] - monitor * wave_ref[1, turn]
        return unused

    lax.fori_loop(0, STEPS, step, 0)
    sent(2)
    sent(3)

    def share(k):
        return pltpu.make_async_remote_copy(
            src_ref=phase,
            dst_ref=gathered.at[me],
            send_sem=gather_send.at[k],
            recv_sem=gather_recv.at[k],
            device_id=peer_at(lax.rem(me + k, count), tiles_y),
            device_id_type=MESH,
        )

    def start(k, unused):
        share(k).start()
        return unused

    lax.fori_loop(1, count, start, 0)

    def store(z, unused):
        for component in range(3):
            final_ref[component, z] = e_ref[component, z]
            final_ref[3 + component, z] = h_ref[component, z + 1]
        return unused

    lax.fori_loop(0, depth, store, 0, unroll=True)

    def finish(k, unused):
        share(k).wait_send()
        share(k).wait_recv()
        return unused

    lax.fori_loop(1, count, finish, 0)
    gathered[me] = phase[...]
    for tile_x in range(tiles_x):
        for tile_y in range(tiles_y):
            phasor_ref[
                :,
                tile_x * cells_x : (tile_x + 1) * cells_x,
                tile_y * cells_y : (tile_y + 1) * cells_y,
            ] = gathered[tile_x * tiles_y + tile_y]


def run_march(fields, material_map, material_eps, material_loss, tiles_x, tiles_y):
    depth, cells_x, cells_y = fields.shape[1:]
    count = tiles_x * tiles_y
    moments = np.float32(ANGULAR) * np.arange(1, STEPS + 1, dtype=np.float32)
    wave = jnp.asarray(np.stack((np.cos(moments), np.sin(moments))).astype(np.float32))
    vmem = pl.BlockSpec(memory_space=pltpu.VMEM)
    smem = pl.BlockSpec(memory_space=pltpu.SMEM)
    state = (3, depth + 1, cells_x, cells_y)
    return pl.pallas_call(
        functools.partial(march, tiles_x, tiles_y),
        out_shape=(
            jax.ShapeDtypeStruct(fields.shape, jnp.float32),
            jax.ShapeDtypeStruct((4, cells_x * tiles_x, cells_y * tiles_y), jnp.float32),
        ),
        in_specs=[vmem, vmem, smem, smem, smem],
        out_specs=(vmem, vmem),
        scratch_shapes=[
            pltpu.VMEM(state, jnp.float32),
            pltpu.VMEM(state, jnp.float32),
            pltpu.VMEM((depth, cells_x, cells_y), jnp.float32),
            pltpu.VMEM((depth, cells_x, cells_y), jnp.float32),
            pltpu.VMEM((2, 2, depth, cells_y), jnp.float32),
            pltpu.VMEM((2, depth, cells_y), jnp.float32),
            pltpu.VMEM((2, depth, cells_y), jnp.float32),
            pltpu.VMEM((2, cells_x, cells_y), jnp.float32),
            pltpu.VMEM((cells_x, cells_y), jnp.float32),
            pltpu.VMEM((cells_x, cells_y), jnp.float32),
            pltpu.VMEM((4, cells_x, cells_y), jnp.float32),
            pltpu.VMEM((count, 4, cells_x, cells_y), jnp.float32),
            pltpu.SemaphoreType.DMA((4,)),
            pltpu.SemaphoreType.DMA((4,)),
            pltpu.SemaphoreType.DMA((count,)),
            pltpu.SemaphoreType.DMA((count,)),
        ],
        compiler_params=pltpu.CompilerParams(
            collective_id=0, has_side_effects=True, vmem_limit_bytes=40 * 1024 * 1024
        ),
    )(fields, material_map, material_eps, material_loss, wave)


def picture(
    tiles_x,
    tiles_y,
    orders_ref,
    shift_ref,
    mask_ref,
    weight_ref,
    rows_ref,
    g_ref,
    image_ref,
    columns,
    part,
    landed,
    send_sem,
    recv_sem,
):
    count = tiles_x * tiles_y
    me = lax.axis_index("gx") * tiles_y + lax.axis_index("gy")
    sources = mask_ref.shape[0]
    size_p = mask_ref.shape[1] // 2
    size_q = mask_ref.shape[2] // 2
    pixels = image_ref.shape[1]
    strip = image_ref.shape[0]
    greet(me, count, tiles_y)

    def one_hot(size, offset, flipped):
        to_id = lax.broadcasted_iota(jnp.int32, (2 * size, 2 * size), 1 if flipped else 0)
        from_id = lax.broadcasted_iota(jnp.int32, (2 * size, 2 * size), 0 if flipped else 1)
        to_half = jnp.where(to_id >= size, size, 0)
        moved = to_id - to_half + offset
        moved = jnp.where(moved < 0, moved + size, moved)
        moved = jnp.where(moved >= size, moved - size, moved)
        return jnp.where(from_id == moved + to_half, 1.0, 0.0).astype(jnp.bfloat16)

    def prepare(source, unused):
        pick_p = one_hot(size_p, shift_ref[source, 0], False)
        pick_q = one_hot(size_q, shift_ref[source, 1], True)
        rolled = jnp.dot(pick_p, orders_ref[...], preferred_element_type=jnp.float32)
        rolled = jnp.dot(
            rolled.astype(jnp.bfloat16), pick_q, preferred_element_type=jnp.float32
        )
        masked = (rolled * mask_ref[source].astype(jnp.float32)).astype(jnp.bfloat16)
        spread = jnp.dot(masked, g_ref[...], preferred_element_type=jnp.float32)
        spread = spread.astype(jnp.bfloat16)
        for block in range(2):
            real = spread[block * size_p : (block + 1) * size_p, :pixels]
            imag = spread[block * size_p : (block + 1) * size_p, pixels:]
            at = 2 * block * pixels
            columns[source, :size_p, at : at + pixels] = real
            columns[source, :size_p, at + pixels : at + 2 * pixels] = imag
            columns[source, size_p:, at : at + pixels] = -imag
            columns[source, size_p:, at + pixels : at + 2 * pixels] = real
        return unused

    lax.fori_loop(0, sources, prepare, 0)

    def copy_to(target, k):
        return pltpu.make_async_remote_copy(
            src_ref=part.at[target],
            dst_ref=landed.at[me],
            send_sem=send_sem.at[k],
            recv_sem=recv_sem.at[k],
            device_id=peer_at(target, tiles_y),
            device_id_type=MESH,
        )

    groups = 4 if count % 4 == 0 else 1
    per_group = count // groups
    high = per_group * strip
    scale = 1.0 / (sources * count)

    def one_group(turn, unused):
        group = lax.rem(me // per_group + 1 + turn, groups)
        table = rows_ref[pl.ds(pl.multiple_of(group * high, high), high), :]

        def add_source(source, running):
            bright = None
            for block in range(4):
                values = jnp.dot(
                    table,
                    columns[source, :, block * pixels : (block + 1) * pixels],
                    preferred_element_type=jnp.float32,
                )
                squared = values * values
                bright = squared if bright is None else bright + squared
            return running + (weight_ref[source] * scale) * bright

        total = lax.fori_loop(
            0, sources, add_source, jnp.zeros((high, pixels), jnp.float32)
        )
        for piece in range(per_group):
            part[group * per_group + piece] = total[piece * strip : (piece + 1) * strip]

        def start(piece, unused):
            target = group * per_group + piece

            @pl.when(target != me)
            def _():
                copy_to(target, lax.rem(target - me + count, count)).start()

            return unused

        return lax.fori_loop(0, per_group, start, unused)

    lax.fori_loop(0, groups, one_group, 0)

    def finish(k, unused):
        copy = copy_to(lax.rem(me + k, count), k)
        copy.wait_send()
        copy.wait_recv()
        return unused

    lax.fori_loop(1, count, finish, 0)
    landed[me] = part[me]

    def add(index, running):
        return running + landed[index]

    image_ref[...] = lax.fori_loop(
        0, count, add, jnp.zeros((strip, pixels), jnp.float32)
    )


def run_picture(orders, shift, mask, weight, row_table, g_matrix, tiles_x, tiles_y):
    count = tiles_x * tiles_y
    pixels = row_table.shape[0]
    strip = pixels // count
    vmem = pl.BlockSpec(memory_space=pltpu.VMEM)
    smem = pl.BlockSpec(memory_space=pltpu.SMEM)
    return pl.pallas_call(
        functools.partial(picture, tiles_x, tiles_y),
        out_shape=jax.ShapeDtypeStruct((strip, pixels), jnp.float32),
        in_specs=[vmem, smem, vmem, smem, vmem, vmem],
        out_specs=vmem,
        scratch_shapes=[
            pltpu.VMEM((mask.shape[0], row_table.shape[1], 4 * pixels), jnp.bfloat16),
            pltpu.VMEM((count, strip, pixels), jnp.float32),
            pltpu.VMEM((count, strip, pixels), jnp.float32),
            pltpu.SemaphoreType.DMA((count,)),
            pltpu.SemaphoreType.DMA((count,)),
        ],
        compiler_params=pltpu.CompilerParams(
            collective_id=1, has_side_effects=True, vmem_limit_bytes=48 * 1024 * 1024
        ),
    )(orders, shift, mask, weight, row_table, g_matrix)


def spectrum(extent, orders, period):
    wrapped = ((np.arange(orders) - orders // 2)[:, None] * np.arange(extent)[None, :]) % period
    angles = 2.0 * math.pi / period * wrapped
    return np.cos(angles).astype(np.float32), np.sin(angles).astype(np.float32)


def image_tables(pixels, orders_p, orders_q):
    cos_u, sin_u = spectrum(pixels, orders_p, pixels)
    row_table = np.concatenate((cos_u.T, sin_u.T), 1) * np.float32(1.0 / math.sqrt(orders_p))
    cos_v, sin_v = spectrum(pixels, orders_q, pixels)
    real_v = cos_v * np.float32(1.0 / math.sqrt(orders_q))
    imag_v = sin_v * np.float32(1.0 / math.sqrt(orders_q))
    g_matrix = np.block([[real_v, imag_v], [-imag_v, real_v]])
    return (row_table.astype(jnp.bfloat16), g_matrix.astype(jnp.bfloat16))


def body(
    fields, material_map, material_eps, material_loss, source_shift, source_mask, source_weight
):
    tiles_x = lax.axis_size("gx")
    tiles_y = lax.axis_size("gy")
    orders_p, orders_q = source_mask.shape[1:]
    final_fields, phasor = run_march(
        fields, material_map, material_eps, material_loss, tiles_x, tiles_y
    )
    period_x, period_y = phasor.shape[1:]
    cos_x, sin_x = spectrum(period_x, orders_p, period_x)
    cos_y, sin_y = spectrum(period_y, orders_q, period_y)
    both_y = jnp.asarray(np.concatenate((cos_y, sin_y), 0).T)
    along = jnp.dot(
        phasor.reshape(4 * period_x, period_y), both_y, precision=PRECISE
    ).reshape(2, 2, period_x, 2 * orders_q)
    part_re = along[0, :, :, :orders_q] + along[1, :, :, orders_q:]
    part_im = along[1, :, :, :orders_q] - along[0, :, :, orders_q:]
    both_x = jnp.asarray(np.concatenate((cos_x, sin_x), 1))
    stacked = jnp.concatenate(
        (
            jnp.concatenate((part_re, part_im), 2),
            jnp.concatenate((part_im, -part_re), 2),
        ),
        1,
    )
    orders = jnp.einsum("px,cxq->cpq", both_x, stacked, precision=PRECISE)
    scaling = 1.0 / math.sqrt(period_x * period_y * STEPS)
    orders_b = (orders * scaling).astype(jnp.bfloat16).reshape(2 * orders_p, 2 * orders_q)
    row_table, g_matrix = image_tables(M, orders_p, orders_q)
    mask = jnp.tile(source_mask.astype(jnp.bfloat16), (1, 2, 2))
    image = run_picture(
        orders_b,
        source_shift,
        mask,
        source_weight,
        jnp.asarray(row_table),
        jnp.asarray(g_matrix),
        tiles_x,
        tiles_y,
    )
    return (final_fields, image)


def solution(mesh):
    placed = (
        P("clips", None, "gx", "gy"),
        P("clips", "gx", "gy"),
        P(),
        P(),
        P(("gx", "gy"), None),
        P(("gx", "gy"), None, None),
        P(("gx", "gy")),
    )
    return jax.shard_map(
        body,
        mesh=mesh,
        in_specs=placed,
        out_specs=(P("clips", None, "gx", "gy"), P(("gx", "gy"), "clips")),
        check_vma=False,
    )
```

time: 470 us -> 139 us (0.30)
  waiting for transfers between devices: 151 us -> 0 us
  Pallas kernels: 0 us -> 129 us
  local copies, waits for them, and re-layouts: 133 us -> 7.69 us
  other arithmetic: 81.8 us -> 0.17 us
  starting transfers between devices: 56.9 us -> 0 us
  matrix products: 23.1 us -> 0.96 us
  between operations: 14.4 us -> 0.75 us
  loops' own time: 6.56 us -> 0 us
    pallas_call x0 -> x2, Pallas kernels: none -> 129 us  [the longest x1 98.9 us: run_march(): pl.pallas_call(functools.partial(march, tiles_x, tiles_y), out_shape=(jax...]
    psum x1 -> x0, waiting for transfers between devices: 92.4 us -> none  [body(): order_re, order_im = lax.psum((order_re, order_im), ('gx', 'gy'))]
    ppermute x20 -> x0, starting transfers between devices: 56.9 us -> none  [the longest x10 44 us: padded_2(): lax.ppermute(tail, axis, [(i, (i + 1) % count) for i in range(ends)])]
    reduce_scatter x1 -> x0, waiting for transfers between devices: 50.6 us -> none  [body(): lax.psum_scatter(lax.fori_loop(0, columns_all.shape[0], add_source, jnp.z...]
    while x61 -> x0, local copies, waits for them, and re-layouts: 39.9 us -> none
    concatenate x9 -> x0, other arithmetic: 24 us -> none  [the longest x8 23.2 us: padded_2(): jnp.concatenate([lax.ppermute(tail, axis, [(i, (i + 1) % count) for i in...]
    slice x152 -> x0, local copies, waits for them, and re-layouts: 23.7 us -> none  [the longest x12 6.36 us: advance_block(): efield = tuple((values[:, 3:-3, 3:-3] for values in e_wide))]
    concatenate x5 -> x0, local copies, waits for them, and re-layouts: 22.2 us -> none  [padded_2(): jnp.concatenate([lax.ppermute(tail, axis, [(i, (i + 1) % count) for i in...]
  transfers between devices with their start and end apart: 22 -> 0, of which waited for: 4 -> 0; matrix products, arithmetic and copies ran while one was open for 13% -> 0% of each run, Pallas kernels for 0% -> 0%
where the time goes in v1:
time: 139 us
  Pallas kernels  129 us (93%)
  local copies, waits for them, and re-layouts  7.69 us (6%)
    pallas_call x1, Pallas kernels, run_march(): pl.pallas_call(functools.partial(march, tiles_x, tiles_y), out_shape=(jax...  98.9 us
    pallas_call x1, Pallas kernels, run_picture(): pl.pallas_call(functools.partial(picture, tiles_x, tiles_y), out_shape=ja...  30.5 us
    unnamed x27, local copies, waits for them, and re-layouts  7.28 us

profile of v1, /device:TPU:0, one launch (start us, length us, event | category | flops | bytes accessed | tf_op | source)
XLA Modules:
  0.0 138.9 jit_solution(1214936623137069316)
XLA Ops:
  0.6 0.0 copy-start.4
  0.6 0.7 copy-done.4
  1.3 0.0 copy-start
  1.3 1.1 copy-done
  2.4 0.0 copy-start.3
  2.4 0.9 copy-done.3
  3.4 0.0 copy-start.5
  3.4 0.7 copy-done.5
  4.0 0.0 copy-start.6
  4.0 0.7 copy-done.6
  4.7 98.9 %shard_map.131 = (f32[6,32,8,128]{3,2,1,0:T(8,128)S(1)}, f32[4,32,512]{2,1,0:T(8,128)S(1)}) custom-call(f32[6,32,8,128]{3,2,1,0:T(8,128)S(1)} %copy-done, s32[32,8,128]{2,1,0:T(8,128)S(1)} %copy-done.3, f32[4]{0:T(128)S(1)} %copy-done.5, f32[4]{0:T(128)S(1)} %copy-done.6, f32[2,12]{1,0:T(2,128)S(1)} %copy-done.4), custom_call_target="tpu_custom_call" | custom-call | tf_op jit(solution)/shard_map/pallas_call | solution.py:292
  103.5 0.0 copy-done.8
  103.6 0.5 fusion.13
  104.1 0.0 copy-start.11
  104.1 0.1 fusion.11
  104.2 0.1 fusion.8
  104.3 0.6 copy-done.11
  104.9 0.4 fusion
  105.3 0.0 copy-done.9
  105.3 0.2 tile.4
  105.5 0.0 copy-start.10
  105.5 0.0 copy-start.1
  105.6 0.0 copy-start.2
  105.6 0.2 tile.10.mask_ref
  105.8 0.4 copy-done.10
  106.2 0.1 copy.14.shift_ref
  106.3 0.2 copy-done.1
  106.6 0.1 copy-done.2
  106.6 0.3 copy-done.7
  106.9 30.5 %shard_map.132 = f32[32,512]{1,0:T(8,128)S(1)} custom-call(bf16[192,192]{1,0:T(8,128)(2,1)S(1)} %bitcast.17, s32[4,2]{1,0:T(4,128)S(1)} %copy.14.shift_ref, bf16[4,192,192]{2,1,0:T(8,128)(2,1)S(1)} %tile.10.mask_ref, f32[4]{0:T(128)S(1)} %copy-done.7, bf16[512,192]{1,0:T(8,128)(2,1)S(1)} %copy-done.2, bf16[192,1024]{1,0:T(8,128)(2,1)S(1)} %copy-done.1), custom_call_target="tpu_custom_call" | custom-call | tf_op jit(solution)/shard_map/pallas_call | solution.py:453
  137.4 0.9 copy.18
  138.3 0.6 copy.19
  (4 shorter events, 0.0 us)
Async XLA Ops:
  0.6 0.7 copy-start.4
  1.3 1.1 copy-start
  2.4 0.9 copy-start.3
  3.4 0.7 copy-start.5
  4.0 0.7 copy-start.6
  4.7 98.9 %copy-start.8 = (f32[512,192,1,1]{0,1,3,2:T(8,128)S(1)}, f32[512,192,1,1]{0,1,3,2:T(8,128)}, u32[]{:S(2)}) copy-start(f32[512,192,1,1]{0,1,3,2:T(8,128)} %constant.20) | copy-start | bytes 1179652
  104.1 0.8 copy-start.11
  104.2 1.1 copy-start.9
  105.5 0.7 copy-start.10
  105.5 1.0 copy-start.1
  105.6 1.1 copy-start.2
  106.2 0.7 copy-start.7

commit v2 on v1

--- a/solution.py
+++ b/solution.py
@@ -15,6 +15,7 @@
 ANGULAR = 0.7
 PRECISE = lax.Precision.HIGHEST
 MESH = pl.DeviceIdType.MESH
+GROUP = 8
 
 
 def peer_at(index, tiles_y):
@@ -172,28 +173,38 @@
             sent(2)
             sent(3)
 
-        def magnetic(z, packed):
-            ex, ey, ez = e_ref[0, z], e_ref[1, z], e_ref[2, z]
-            ex_up, ey_up = e_ref[0, z + 1], e_ref[1, z + 1]
-            row_z = jnp.broadcast_to(row_e[0, pl.ds(z, 1), :], tile)
-            row_y = jnp.broadcast_to(row_e[1, pl.ds(z, 1), :], tile)
-            col_z = pltpu.roll(edge, cells_y - 1 - z, 1)
-            col_x = pltpu.roll(edge, cells_y - 1 - depth - z, 1)
-            dx_ez = jnp.where(last_row, row_z, pltpu.roll(ez, cells_x - 1, 0)) - ez
-            dx_ey = jnp.where(last_row, row_y, pltpu.roll(ey, cells_x - 1, 0)) - ey
-            dy_ez = jnp.where(last_col, col_z, pltpu.roll(ez, cells_y - 1, 1)) - ez
-            dy_ex = jnp.where(last_col, col_x, pltpu.roll(ex, cells_y - 1, 1)) - ex
-            hx = h_ref[0, z + 1] - COURANT * (dy_ez - (ey_up - ey))
-            hy = h_ref[1, z + 1] - COURANT * ((ex_up - ex) - dx_ez)
-            hz = h_ref[2, z + 1] - COURANT * (dx_ey - dy_ex)
-            h_ref[0, z + 1] = hx
-            h_ref[1, z + 1] = hy
-            h_ref[2, z + 1] = hz
-            row_out[1, 0, pl.ds(z, 1), :] = hz[cells_x - 1 : cells_x]
-            row_out[1, 1, pl.ds(z, 1), :] = hy[cells_x - 1 : cells_x]
-            return pack_columns(packed, z, hz, hx, cells_y - 1)
-
-        col_out[1] = lax.fori_loop(0, depth, magnetic, blank, unroll=True)
+        def magnetic(block, packed):
+            base = block * GROUP
+            ex = [e_ref[0, base + j] for j in range(GROUP + 1)]
+            ey = [e_ref[1, base + j] for j in range(GROUP + 1)]
+            ez = [e_ref[2, base + j] for j in range(GROUP)]
+            new = []
+            for j in range(GROUP):
+                z = base + j
+                row_z = jnp.broadcast_to(row_e[0, pl.ds(z, 1), :], tile)
+                row_y = jnp.broadcast_to(row_e[1, pl.ds(z, 1), :], tile)
+                col_z = pltpu.roll(edge, cells_y - 1 - z, 1)
+                col_x = pltpu.roll(edge, cells_y - 1 - depth - z, 1)
+                dx_ez = jnp.where(last_row, row_z, pltpu.roll(ez[j], cells_x - 1, 0)) - ez[j]
+                dx_ey = jnp.where(last_row, row_y, pltpu.roll(ey[j], cells_x - 1, 0)) - ey[j]
+                dy_ez = jnp.where(last_col, col_z, pltpu.roll(ez[j], cells_y - 1, 1)) - ez[j]
+                dy_ex = jnp.where(last_col, col_x, pltpu.roll(ex[j], cells_y - 1, 1)) - ex[j]
+                hx = h_ref[0, z + 1] - COURANT * (dy_ez - (ey[j + 1] - ey[j]))
+                hy = h_ref[1, z + 1] - COURANT * ((ex[j + 1] - ex[j]) - dx_ez)
+                hz = h_ref[2, z + 1] - COURANT * (dx_ey - dy_ex)
+                new.append((hx, hy, hz))
+            for j in range(GROUP):
+                z = base + j
+                hx, hy, hz = new[j]
+                h_ref[0, z + 1] = hx
+                h_ref[1, z + 1] = hy
+                h_ref[2, z + 1] = hz
+                row_out[1, 0, pl.ds(z, 1), :] = hz[cells_x - 1 : cells_x]
+                row_out[1, 1, pl.ds(z, 1), :] = hy[cells_x - 1 : cells_x]
+                packed = pack_columns(packed, z, hz, hx, cells_y - 1)
+            return packed
+
+        col_out[1] = lax.fori_loop(0, depth // GROUP, magnetic, blank, unroll=True)
         send(2)
         send(3)
         sent(0)
@@ -202,29 +213,39 @@
         arrived(3)
         edge = col_h[...]
 
-        def electric(z, packed):
-            hx, hy, hz = h_ref[0, z + 1], h_ref[1, z + 1], h_ref[2, z + 1]
-            hx_down, hy_down = h_ref[0, z], h_ref[1, z]
-            row_z = jnp.broadcast_to(row_h[0, pl.ds(z, 1), :], tile)
-            row_y = jnp.broadcast_to(row_h[1, pl.ds(z, 1), :], tile)
-            col_z = pltpu.roll(edge, lax.rem(cells_y - z, cells_y), 1)
-            col_x = pltpu.roll(edge, cells_y - depth - z, 1)
-            dx_hz = hz - jnp.where(first_row, row_z, pltpu.roll(hz, 1, 0))
-            dx_hy = hy - jnp.where(first_row, row_y, pltpu.roll(hy, 1, 0))
-            dy_hz = hz - jnp.where(first_col, col_z, pltpu.roll(hz, 1, 1))
-            dy_hx = hx - jnp.where(first_col, col_x, pltpu.roll(hx, 1, 1))
-            keep, curl = keep_ref[z], curl_ref[z]
-            ex = keep * e_ref[0, z] + curl * (dy_hz - (hy - hy_down))
-            ey = keep * e_ref[1, z] + curl * ((hx - hx_down) - dx_hz)
-            ez = keep * e_ref[2, z] + curl * (dx_hy - dy_hx)
-            e_ref[0, z] = ex
-            e_ref[1, z] = ey
-            e_ref[2, z] = ez
-            row_out[0, 0, pl.ds(z, 1), :] = ez[0:1]
-            row_out[0, 1, pl.ds(z, 1), :] = ey[0:1]
-            return pack_columns(packed, z, ez, ex, 0)
-
-        col_out[0] = lax.fori_loop(0, depth, electric, blank, unroll=True)
+        def electric(block, packed):
+            base = block * GROUP
+            hx = [h_ref[0, base + j] for j in range(GROUP + 1)]
+            hy = [h_ref[1, base + j] for j in range(GROUP + 1)]
+            hz = [None] + [h_ref[2, base + j + 1] for j in range(GROUP)]
+            new = []
+            for j in range(1, GROUP + 1):
+                z = base + j - 1
+                row_z = jnp.broadcast_to(row_h[0, pl.ds(z, 1), :], tile)
+                row_y = jnp.broadcast_to(row_h[1, pl.ds(z, 1), :], tile)
+                col_z = pltpu.roll(edge, lax.rem(cells_y - z, cells_y), 1)
+                col_x = pltpu.roll(edge, cells_y - depth - z, 1)
+                dx_hz = hz[j] - jnp.where(first_row, row_z, pltpu.roll(hz[j], 1, 0))
+                dx_hy = hy[j] - jnp.where(first_row, row_y, pltpu.roll(hy[j], 1, 0))
+                dy_hz = hz[j] - jnp.where(first_col, col_z, pltpu.roll(hz[j], 1, 1))
+                dy_hx = hx[j] - jnp.where(first_col, col_x, pltpu.roll(hx[j], 1, 1))
+                keep, curl = keep_ref[z], curl_ref[z]
+                ex = keep * e_ref[0, z] + curl * (dy_hz - (hy[j] - hy[j - 1]))
+                ey = keep * e_ref[1, z] + curl * ((hx[j] - hx[j - 1]) - dx_hz)
+                ez = keep * e_ref[2, z] + curl * (dx_hy - dy_hx)
+                new.append((ex, ey, ez))
+            for j in range(GROUP):
+                z = base + j
+                ex, ey, ez = new[j]
+                e_ref[0, z] = ex
+                e_ref[1, z] = ey
+                e_ref[2, z] = ez
+                row_out[0, 0, pl.ds(z, 1), :] = ez[0:1]
+                row_out[0, 1, pl.ds(z, 1), :] = ey[0:1]
+                packed = pack_columns(packed, z, ez, ex, 0)
+            return packed
+
+        col_out[0] = lax.fori_loop(0, depth // GROUP, electric, blank, unroll=True)
 
         @pl.when(turn < STEPS - 1)
         def _():
@@ -333,9 +354,16 @@
     image_ref,
     columns,
     part,
+    swapped,
+    crossed,
+    strips,
     landed,
-    send_sem,
-    recv_sem,
+    swap_send,
+    swap_recv,
+    cross_send,
+    cross_recv,
+    hand_send,
+    hand_recv,
 ):
     count = tiles_x * tiles_y
     me = lax.axis_index("gx") * tiles_y + lax.axis_index("gy")
@@ -377,26 +405,20 @@
 
     lax.fori_loop(0, sources, prepare, 0)
 
-    def copy_to(target, k):
-        return pltpu.make_async_remote_copy(
-            src_ref=part.at[target],
-            dst_ref=landed.at[me],
-            send_sem=send_sem.at[k],
-            recv_sem=recv_sem.at[k],
-            device_id=peer_at(target, tiles_y),
-            device_id_type=MESH,
-        )
-
-    groups = 4 if count % 4 == 0 else 1
-    per_group = count // groups
-    high = per_group * strip
+    pairs = tiles_x // 2
+    at_x = lax.axis_index("gx")
+    at_y = lax.axis_index("gy")
+    core = lax.rem(at_x, 2)
+    at_pair = at_x // 2
     scale = 1.0 / (sources * count)
-
-    def one_group(turn, unused):
-        group = lax.rem(me // per_group + 1 + turn, groups)
-        table = rows_ref[pl.ds(pl.multiple_of(group * high, high), high), :]
-
-        def add_source(source, running):
+    high = tiles_y * strip
+
+    def render(pair, half):
+        table = rows_ref[
+            pl.ds(pl.multiple_of((2 * pair + half) * high, high), high), :
+        ]
+        total = jnp.zeros((high, pixels), jnp.float32)
+        for source in range(sources):
             bright = None
             for block in range(4):
                 values = jnp.dot(
@@ -406,48 +428,101 @@
                 )
                 squared = values * values
                 bright = squared if bright is None else bright + squared
-            return running + (weight_ref[source] * scale) * bright
-
-        total = lax.fori_loop(
-            0, sources, add_source, jnp.zeros((high, pixels), jnp.float32)
-        )
-        for piece in range(per_group):
-            part[group * per_group + piece] = total[piece * strip : (piece + 1) * strip]
-
-        def start(piece, unused):
-            target = group * per_group + piece
-
-            @pl.when(target != me)
-            def _():
-                copy_to(target, lax.rem(target - me + count, count)).start()
-
-            return unused
-
-        return lax.fori_loop(0, per_group, start, unused)
-
-    lax.fori_loop(0, groups, one_group, 0)
-
-    def finish(k, unused):
-        copy = copy_to(lax.rem(me + k, count), k)
-        copy.wait_send()
-        copy.wait_recv()
-        return unused
-
-    lax.fori_loop(1, count, finish, 0)
-    landed[me] = part[me]
-
-    def add(index, running):
-        return running + landed[index]
-
-    image_ref[...] = lax.fori_loop(
-        0, count, add, jnp.zeros((strip, pixels), jnp.float32)
-    )
+            total = total + (weight_ref[source] * scale) * bright
+        part[pair, half] = total
+
+    def swap(pair):
+        return pltpu.make_async_remote_copy(
+            src_ref=part.at[pair, 1 - core],
+            dst_ref=swapped.at[pair],
+            send_sem=swap_send.at[pair],
+            recv_sem=swap_recv.at[pair],
+            device_id={"gx": at_x + 1 - 2 * core},
+            device_id_type=MESH,
+        )
+
+    def cross(k):
+        pair = lax.rem(at_pair + k, pairs)
+        return pltpu.make_async_remote_copy(
+            src_ref=part.at[pair, core],
+            dst_ref=crossed.at[k],
+            send_sem=cross_send.at[k],
+            recv_sem=cross_recv.at[k],
+            device_id={"gx": 2 * pair + core},
+            device_id_type=MESH,
+        )
+
+    def away(k):
+        return lax.rem(at_pair + k, pairs)
+
+    def first(turn, unused):
+        pair = away(turn + 1)
+        render(pair, 1 - core)
+        swap(pair).start()
+        render(pair, core)
+        return unused
+
+    lax.fori_loop(0, pairs, first, 0)
+
+    def second(turn, unused):
+        pair = away(turn + 1)
+        swap(pair).wait_recv()
+        part[pair, core] = part[pair, core] + swapped[pair]
+
+        @pl.when(turn < pairs - 1)
+        def _():
+            cross(turn + 1).start()
+
+        return unused
+
+    lax.fori_loop(0, pairs, second, 0)
+
+    def gather_pairs(k, running):
+        cross(k).wait_recv()
+        return running + crossed[k]
+
+    mine = lax.fori_loop(1, pairs, gather_pairs, part[at_pair, core])
+    for owner in range(tiles_y):
+        strips[owner] = mine[owner * strip : (owner + 1) * strip]
+
+    def hand(k):
+        owner = lax.rem(at_y + k, tiles_y)
+        return pltpu.make_async_remote_copy(
+            src_ref=strips.at[owner],
+            dst_ref=landed.at[k],
+            send_sem=hand_send.at[k],
+            recv_sem=hand_recv.at[k],
+            device_id={"gy": owner},
+            device_id_type=MESH,
+        )
+
+    for k in range(1, tiles_y):
+        hand(k).start()
+    total = strips[at_y]
+    for k in range(1, tiles_y):
+        hand(k).wait_recv()
+        total = total + landed[k]
+    image_ref[...] = total
+    for k in range(1, tiles_y):
+        hand(k).wait_send()
+
+    def finish(pair, unused):
+        swap(pair).wait_send()
+
+        @pl.when(pair > 0)
+        def _():
+            cross(pair).wait_send()
+
+        return unused
+
+    lax.fori_loop(0, pairs, finish, 0)
 
 
 def run_picture(orders, shift, mask, weight, row_table, g_matrix, tiles_x, tiles_y):
     count = tiles_x * tiles_y
     pixels = row_table.shape[0]
     strip = pixels // count
+    pairs = tiles_x // 2
     vmem = pl.BlockSpec(memory_space=pltpu.VMEM)
     smem = pl.BlockSpec(memory_space=pltpu.SMEM)
     return pl.pallas_call(
@@ -457,11 +532,14 @@
         out_specs=vmem,
         scratch_shapes=[
             pltpu.VMEM((mask.shape[0], row_table.shape[1], 4 * pixels), jnp.bfloat16),
-            pltpu.VMEM((count, strip, pixels), jnp.float32),
-            pltpu.VMEM((count, strip, pixels), jnp.float32),
-            pltpu.SemaphoreType.DMA((count,)),
-            pltpu.SemaphoreType.DMA((count,)),
-        ],
+            pltpu.VMEM((pairs, 2, tiles_y * strip, pixels), jnp.float32),
+            pltpu.VMEM((pairs, tiles_y * strip, pixels), jnp.float32),
+            pltpu.VMEM((pairs, tiles_y * strip, pixels), jnp.float32),
+            pltpu.VMEM((tiles_y, strip, pixels), jnp.float32),
+            pltpu.VMEM((tiles_y, strip, pixels), jnp.float32),
+        ]
+        + [pltpu.SemaphoreType.DMA((pairs,))] * 4
+        + [pltpu.SemaphoreType.DMA((tiles_y,))] * 2,
         compiler_params=pltpu.CompilerParams(
             collective_id=1, has_side_effects=True, vmem_limit_bytes=48 * 1024 * 1024
         ),

time: 139 us -> 119 us (0.86)
  Pallas kernels: 129 us -> 109 us
    pallas_call x1, Pallas kernels: 98.9 us -> 86.4 us  [run_march(): pl.pallas_call(functools.partial(march, tiles_x, tiles_y), out_shape=(jax...]
    pallas_call x1, Pallas kernels: 30.5 us -> 22.5 us  [run_picture(): pl.pallas_call(functools.partial(picture, tiles_x, tiles_y), out_shape=ja...]
where the time goes in v2:
time: 119 us; the launch traced here: 118 us
  Pallas kernels  109 us (92%)
  local copies, waits for them, and re-layouts  7.69 us (6%)
    pallas_call x1, Pallas kernels, run_march(): pl.pallas_call(functools.partial(march, tiles_x, tiles_y), out_shape=(jax...  86.4 us
    pallas_call x1, Pallas kernels, run_picture(): pl.pallas_call(functools.partial(picture, tiles_x, tiles_y), out_shape=ja...  22.5 us
    unnamed x27, local copies, waits for them, and re-layouts  7.28 us

profile of v2, /device:TPU:0, one launch (start us, length us, event | category | flops | bytes accessed | tf_op | source)
XLA Modules:
  0.0 118.5 jit_solution(6296877924721911168)
XLA Ops:
  0.6 0.0 copy-start.4
  0.6 0.7 copy-done.4
  1.3 0.0 copy-start
  1.3 1.1 copy-done
  2.4 0.0 copy-start.3
  2.4 0.9 copy-done.3
  3.4 0.0 copy-start.5
  3.4 0.7 copy-done.5
  4.0 0.0 copy-start.6
  4.0 0.7 copy-done.6
  4.7 86.4 %shard_map.131 = (f32[6,32,8,128]{3,2,1,0:T(8,128)S(1)}, f32[4,32,512]{2,1,0:T(8,128)S(1)}) custom-call(f32[6,32,8,128]{3,2,1,0:T(8,128)S(1)} %copy-done, s32[32,8,128]{2,1,0:T(8,128)S(1)} %copy-done.3, f32[4]{0:T(128)S(1)} %copy-done.5, f32[4]{0:T(128)S(1)} %copy-done.6, f32[2,12]{1,0:T(2,128)S(1)} %copy-done.4), custom_call_target="tpu_custom_call" | custom-call | tf_op jit(solution)/shard_map/pallas_call | solution.py:313
  91.1 0.0 copy-done.8
  91.1 0.5 fusion.13
  91.7 0.0 copy-start.11
  91.7 0.1 fusion.11
  91.8 0.1 fusion.8
  91.8 0.6 copy-done.11
  92.4 0.4 fusion
  92.9 0.0 copy-done.9
  92.9 0.2 tile.4
  93.1 0.0 copy-start.10
  93.1 0.0 copy-start.1
  93.1 0.0 copy-start.2
  93.1 0.2 tile.10.mask_ref
  93.4 0.4 copy-done.10
  93.8 0.1 copy.14.shift_ref
  93.9 0.2 copy-done.1
  94.1 0.1 copy-done.2
  94.2 0.3 copy-done.7
  94.5 22.5 %shard_map.132 = f32[32,512]{1,0:T(8,128)S(1)} custom-call(bf16[192,192]{1,0:T(8,128)(2,1)S(1)} %bitcast.17, s32[4,2]{1,0:T(4,128)S(1)} %copy.14.shift_ref, bf16[4,192,192]{2,1,0:T(8,128)(2,1)S(1)} %tile.10.mask_ref, f32[4]{0:T(128)S(1)} %copy-done.7, bf16[512,192]{1,0:T(8,128)(2,1)S(1)} %copy-done.2, bf16[192,1024]{1,0:T(8,128)(2,1)S(1)} %copy-done.1), custom_call_target="tpu_custom_call" | custom-call | tf_op jit(solution)/shard_map/pallas_call | solution.py:528
  117.0 0.9 copy.18
  117.8 0.6 copy.19
  (4 shorter events, 0.0 us)
Async XLA Ops:
  0.6 0.7 copy-start.4
  1.3 1.1 copy-start
  2.4 0.9 copy-start.3
  3.4 0.7 copy-start.5
  4.0 0.7 copy-start.6
  4.7 86.4 %copy-start.8 = (f32[512,192,1,1]{0,1,3,2:T(8,128)S(1)}, f32[512,192,1,1]{0,1,3,2:T(8,128)}, u32[]{:S(2)}) copy-start(f32[512,192,1,1]{0,1,3,2:T(8,128)} %constant.20) | copy-start | bytes 1179652
  91.7 0.8 copy-start.11
  91.8 1.1 copy-start.9
  93.1 0.7 copy-start.10
  93.1 1.0 copy-start.1
  93.1 1.1 copy-start.2
  93.8 0.7 copy-start.7

commit v3 on v2

--- a/solution.py
+++ b/solution.py
@@ -58,6 +58,12 @@
     col_out,
     col_e,
     col_h,
+    row_g,
+    col_g,
+    row_d,
+    col_d,
+    row_far,
+    col_far,
     phase,
     gathered,
     send_sem,
@@ -84,40 +90,58 @@
     has_left_x = at_x > 0
     has_right_y = at_y < tiles_y - 1
     has_left_y = at_y > 0
+    x_up, x_down = {"gx": at_x + 1}, {"gx": at_x - 1}
+    y_up, y_down = {"gy": at_y + 1}, {"gy": at_y - 1}
     routes = (
-        (row_out.at[0], row_e, {"gx": at_x - 1}, has_left_x, has_right_x),
-        (col_out.at[0], col_e, {"gy": at_y - 1}, has_left_y, has_right_y),
-        (row_out.at[1], row_h, {"gx": at_x + 1}, has_right_x, has_left_x),
-        (col_out.at[1], col_h, {"gy": at_y + 1}, has_right_y, has_left_y),
+        (row_out.at[0], row_e, x_down, has_left_x, has_right_x),
+        (col_out.at[0], col_e, y_down, has_left_y, has_right_y),
+        (row_far, row_g, x_up, has_right_x, has_left_x),
+        (col_far, col_g, y_up, has_right_y, has_left_y),
+        (
+            row_far.at[2],
+            row_d,
+            {"gx": at_x + 1, "gy": at_y - 1},
+            has_right_x & has_left_y,
+            has_left_x & has_right_y,
+        ),
+        (
+            col_far,
+            col_d,
+            {"gx": at_x - 1, "gy": at_y + 1},
+            has_left_x & has_right_y,
+            has_right_x & has_left_y,
+        ),
+        (row_out.at[1], row_h, x_up, has_right_x, has_left_x),
+        (col_out.at[1], col_h, y_up, has_right_y, has_left_y),
     )
 
-    def copy_of(slot):
+    def copy_of(slot, odd):
         source, target, device, _, _ = routes[slot]
         return pltpu.make_async_remote_copy(
             src_ref=source,
-            dst_ref=target,
+            dst_ref=target if slot > 5 else target.at[odd],
             send_sem=send_sem.at[slot],
-            recv_sem=recv_sem.at[slot],
+            recv_sem=recv_sem.at[slot, odd],
             device_id=device,
             device_id_type=MESH,
         )
 
-    def send(slot):
+    def send(slot, odd):
         @pl.when(routes[slot][3])
         def _():
-            copy_of(slot).start()
-
-    def sent(slot):
+            copy_of(slot, odd).start()
+
+    def sent(slot, odd):
         @pl.when(routes[slot][3])
         def _():
-            copy_of(slot).wait_send()
-
-    def arrived(slot):
+            copy_of(slot, odd).wait_send()
+
+    def arrived(slot, odd):
         @pl.when(routes[slot][4])
         def _():
-            copy_of(slot).wait_recv()
-
-    for halo in (row_e, row_h, col_e, col_h):
+            copy_of(slot, odd).wait_recv()
+
+    for halo in (row_e, row_h, col_e, col_h, row_g, col_g, row_d, col_d):
         halo[...] = jnp.zeros(halo.shape, jnp.float32)
     greet(me, count, tiles_y)
 
@@ -143,35 +167,89 @@
             packed,
         )
 
-    def load(z, packed):
-        materials = material_ref[z]
-        keep = keep_values[0]
-        curl = curl_values[0]
-        for material in range(1, len(keep_values)):
-            keep = jnp.where(materials == material, keep_values[material], keep)
-            curl = jnp.where(materials == material, curl_values[material], curl)
-        keep_ref[z] = keep
-        curl_ref[z] = curl
-        for component in range(3):
-            e_ref[component, z] = fields_ref[component, z]
-            h_ref[component, z + 1] = fields_ref[3 + component, z]
-        row_out[0, 0, pl.ds(z, 1), :] = fields_ref[2, z][0:1]
-        row_out[0, 1, pl.ds(z, 1), :] = fields_ref[1, z][0:1]
-        return pack_columns(packed, z, fields_ref[2, z], fields_ref[0, z], 0)
-
-    col_out[0] = lax.fori_loop(0, depth, load, blank, unroll=True)
-    send(0)
-    send(1)
+    def edges(z, ex, ey, ez, near, far):
+        row_out[0, 0, pl.ds(z, 1), :] = ez[0:1]
+        row_out[0, 1, pl.ds(z, 1), :] = ey[0:1]
+        for place, values in enumerate((ez, ey, ex)):
+            row_far[place, pl.ds(z, 1), :] = values[cells_x - 1 : cells_x]
+        near = pack_columns(near, z, ez, ex, 0)
+        far = pack_columns(far, z, ez, ex, cells_y - 1)
+        far = jnp.where(
+            col_id == 2 * depth + z,
+            jnp.broadcast_to(ey[:, cells_y - 1 : cells_y], tile),
+            far,
+        )
+        return near, far
+
+    def load(block, packed):
+        near, far, beyond = packed
+        base = block * GROUP
+        new = []
+        for j in range(GROUP):
+            materials = material_ref[base + j]
+            keep = keep_values[0]
+            curl = curl_values[0]
+            for material in range(1, len(keep_values)):
+                keep = jnp.where(materials == material, keep_values[material], keep)
+                curl = jnp.where(materials == material, curl_values[material], curl)
+            new.append((keep, curl, [fields_ref[c, base + j] for c in range(6)]))
+        for j in range(GROUP):
+            z = base + j
+            keep_ref[z], curl_ref[z] = new[j][:2]
+            values = new[j][2]
+            for component in range(3):
+                e_ref[component, z] = values[component]
+                h_ref[component, z + 1] = values[3 + component]
+            near, far = edges(z, values[0], values[1], values[2], near, far)
+            row_out[1, 0, pl.ds(z, 1), :] = values[5][cells_x - 1 : cells_x]
+            row_out[1, 1, pl.ds(z, 1), :] = values[4][cells_x - 1 : cells_x]
+            beyond = pack_columns(beyond, z, values[5], values[3], cells_y - 1)
+        return near, far, beyond
+
+    col_out[0], col_far[...], col_out[1] = lax.fori_loop(
+        0, depth // GROUP, load, (blank, blank, blank), unroll=True
+    )
+    for slot in range(8):
+        send(slot, 0)
+    for slot in (6, 7):
+        arrived(slot, 0)
+
+    plane = (depth, cells_y)
+    depth_id = lax.broadcasted_iota(jnp.int32, plane, 0)
+    plane_col = lax.broadcasted_iota(jnp.int32, plane, 1)
+    keep_x = jnp.where(has_left_x, COURANT, 0.0)
+    keep_y = jnp.where(has_left_y, COURANT, 0.0)
+
+    def beyond_edges(odd):
+        ez_g, ey_g, ex_g = row_g[odd, 0], row_g[odd, 1], row_g[odd, 2]
+        ex_next = jnp.where(
+            plane_col == cells_y - 1,
+            pltpu.roll(row_d[odd], cells_y - 1, 1),
+            pltpu.roll(ex_g, cells_y - 1, 1),
+        )
+        ex_up = jnp.where(depth_id == depth - 1, 0.0, pltpu.roll(ex_g, depth - 1, 0))
+        row_h[0] = row_h[0] - keep_x * ((row_out[0, 1] - ey_g) - (ex_next - ex_g))
+        row_h[1] = row_h[1] - keep_x * ((ex_up - ex_g) - (row_out[0, 0] - ez_g))
+
+        near, far = col_out[0], col_g[odd]
+        ahead = jnp.where(
+            last_row, pltpu.roll(col_d[odd], cells_x - 1, 0), pltpu.roll(far, cells_x - 1, 0)
+        )
+        change = near - far
+        dx_ey = pltpu.roll(ahead - far, cells_y - 2 * depth, 1)
+        dy_ex = pltpu.roll(change, cells_y - depth, 1)
+        up = jnp.where(col_id == 3 * depth - 1, 0.0, pltpu.roll(far, cells_y - 1, 1))
+        dz_ey = pltpu.roll(up - far, cells_y - depth, 1)
+        dy_ez = pltpu.roll(change, depth, 1)
+        col_h[...] = col_h[...] - keep_y * jnp.where(
+            col_id < depth, dx_ey - dy_ex, dy_ez - dz_ey
+        )
 
     def step(turn, unused):
-        arrived(0)
-        arrived(1)
-        edge = col_e[...]
-
-        @pl.when(turn > 0)
-        def _():
-            sent(2)
-            sent(3)
+        odd = lax.rem(turn, 2)
+        for slot in range(6):
+            arrived(slot, odd)
+        edge = col_e[odd]
 
         def magnetic(block, packed):
             base = block * GROUP
@@ -181,8 +259,8 @@
             new = []
             for j in range(GROUP):
                 z = base + j
-                row_z = jnp.broadcast_to(row_e[0, pl.ds(z, 1), :], tile)
-                row_y = jnp.broadcast_to(row_e[1, pl.ds(z, 1), :], tile)
+                row_z = jnp.broadcast_to(row_e[odd, 0, pl.ds(z, 1), :], tile)
+                row_y = jnp.broadcast_to(row_e[odd, 1, pl.ds(z, 1), :], tile)
                 col_z = pltpu.roll(edge, cells_y - 1 - z, 1)
                 col_x = pltpu.roll(edge, cells_y - 1 - depth - z, 1)
                 dx_ez = jnp.where(last_row, row_z, pltpu.roll(ez[j], cells_x - 1, 0)) - ez[j]
@@ -199,21 +277,16 @@
                 h_ref[0, z + 1] = hx
                 h_ref[1, z + 1] = hy
                 h_ref[2, z + 1] = hz
-                row_out[1, 0, pl.ds(z, 1), :] = hz[cells_x - 1 : cells_x]
-                row_out[1, 1, pl.ds(z, 1), :] = hy[cells_x - 1 : cells_x]
-                packed = pack_columns(packed, z, hz, hx, cells_y - 1)
             return packed
 
-        col_out[1] = lax.fori_loop(0, depth // GROUP, magnetic, blank, unroll=True)
-        send(2)
-        send(3)
-        sent(0)
-        sent(1)
-        arrived(2)
-        arrived(3)
-        edge = col_h[...]
+        lax.fori_loop(0, depth // GROUP, magnetic, 0, unroll=True)
+        beyond_edges(odd)
+        for slot in range(6):
+            sent(slot, odd)
+        edge_h = col_h[...]
 
         def electric(block, packed):
+            near, far = packed
             base = block * GROUP
             hx = [h_ref[0, base + j] for j in range(GROUP + 1)]
             hy = [h_ref[1, base + j] for j in range(GROUP + 1)]
@@ -223,8 +296,8 @@
                 z = base + j - 1
                 row_z = jnp.broadcast_to(row_h[0, pl.ds(z, 1), :], tile)
                 row_y = jnp.broadcast_to(row_h[1, pl.ds(z, 1), :], tile)
-                col_z = pltpu.roll(edge, lax.rem(cells_y - z, cells_y), 1)
-                col_x = pltpu.roll(edge, cells_y - depth - z, 1)
+                col_z = pltpu.roll(edge_h, lax.rem(cells_y - z, cells_y), 1)
+                col_x = pltpu.roll(edge_h, cells_y - depth - z, 1)
                 dx_hz = hz[j] - jnp.where(first_row, row_z, pltpu.roll(hz[j], 1, 0))
                 dx_hy = hy[j] - jnp.where(first_row, row_y, pltpu.roll(hy[j], 1, 0))
                 dy_hz = hz[j] - jnp.where(first_col, col_z, pltpu.roll(hz[j], 1, 1))
@@ -240,17 +313,17 @@
                 e_ref[0, z] = ex
                 e_ref[1, z] = ey
                 e_ref[2, z] = ez
-                row_out[0, 0, pl.ds(z, 1), :] = ez[0:1]
-                row_out[0, 1, pl.ds(z, 1), :] = ey[0:1]
-                packed = pack_columns(packed, z, ez, ex, 0)
-            return packed
-
-        col_out[0] = lax.fori_loop(0, depth // GROUP, electric, blank, unroll=True)
+                near, far = edges(z, ex, ey, ez, near, far)
+            return near, far
+
+        col_out[0], col_far[...] = lax.fori_loop(
+            0, depth // GROUP, electric, (blank, blank), unroll=True
+        )
 
         @pl.when(turn < STEPS - 1)
         def _():
-            send(0)
-            send(1)
+            for slot in range(6):
+                send(slot, 1 - odd)
 
         for component in range(2):
             monitor = e_ref[component, middle]
@@ -259,8 +332,8 @@
         return unused
 
     lax.fori_loop(0, STEPS, step, 0)
-    sent(2)
-    sent(3)
+    for slot in (6, 7):
+        sent(slot, 0)
 
     def share(k):
         return pltpu.make_async_remote_copy(
@@ -278,13 +351,19 @@
 
     lax.fori_loop(1, count, start, 0)
 
-    def store(z, unused):
-        for component in range(3):
-            final_ref[component, z] = e_ref[component, z]
-            final_ref[3 + component, z] = h_ref[component, z + 1]
-        return unused
-
-    lax.fori_loop(0, depth, store, 0, unroll=True)
+    def store(block, unused):
+        base = block * GROUP
+        values = [
+            [e_ref[component, base + j] for component in range(3)]
+            + [h_ref[component, base + j + 1] for component in range(3)]
+            for j in range(GROUP)
+        ]
+        for j in range(GROUP):
+            for component in range(6):
+                final_ref[component, base + j] = values[j][component]
+        return unused
+
+    lax.fori_loop(0, depth // GROUP, store, 0, unroll=True)
 
     def finish(k, unused):
         share(k).wait_send()
@@ -324,15 +403,21 @@
             pltpu.VMEM((depth, cells_x, cells_y), jnp.float32),
             pltpu.VMEM((depth, cells_x, cells_y), jnp.float32),
             pltpu.VMEM((2, 2, depth, cells_y), jnp.float32),
-            pltpu.VMEM((2, depth, cells_y), jnp.float32),
+            pltpu.VMEM((2, 2, depth, cells_y), jnp.float32),
             pltpu.VMEM((2, depth, cells_y), jnp.float32),
             pltpu.VMEM((2, cells_x, cells_y), jnp.float32),
+            pltpu.VMEM((2, cells_x, cells_y), jnp.float32),
             pltpu.VMEM((cells_x, cells_y), jnp.float32),
+            pltpu.VMEM((2, 3, depth, cells_y), jnp.float32),
+            pltpu.VMEM((2, cells_x, cells_y), jnp.float32),
+            pltpu.VMEM((2, depth, cells_y), jnp.float32),
+            pltpu.VMEM((2, cells_x, cells_y), jnp.float32),
+            pltpu.VMEM((3, depth, cells_y), jnp.float32),
             pltpu.VMEM((cells_x, cells_y), jnp.float32),
             pltpu.VMEM((4, cells_x, cells_y), jnp.float32),
             pltpu.VMEM((count, 4, cells_x, cells_y), jnp.float32),
-            pltpu.SemaphoreType.DMA((4,)),
-            pltpu.SemaphoreType.DMA((4,)),
+            pltpu.SemaphoreType.DMA((8,)),
+            pltpu.SemaphoreType.DMA((8, 2)),
             pltpu.SemaphoreType.DMA((count,)),
             pltpu.SemaphoreType.DMA((count,)),
         ],

time: 119 us -> 91.6 us (0.77)
  Pallas kernels: 109 us -> 81.7 us
    pallas_call x1, Pallas kernels: 86.4 us -> 58.9 us  [run_march(): pl.pallas_call(functools.partial(march, tiles_x, tiles_y), out_shape=(jax...]
where the time goes in v3:
time: 91.6 us; the launch traced here: 91.3 us
  Pallas kernels  81.7 us (89%)
  local copies, waits for them, and re-layouts  7.69 us (8%)
  matrix products  0.97 us (1%)
    pallas_call x1, Pallas kernels, run_march(): pl.pallas_call(functools.partial(march, tiles_x, tiles_y), out_shape=(jax...  58.9 us
    pallas_call x1, Pallas kernels, run_picture(): pl.pallas_call(functools.partial(picture, tiles_x, tiles_y), out_shape=ja...  22.8 us
    unnamed x27, local copies, waits for them, and re-layouts  7.28 us

profile of v3, /device:TPU:0, one launch (start us, length us, event | category | flops | bytes accessed | tf_op | source)
XLA Modules:
  0.0 91.3 jit_solution(18435070252777204661)
XLA Ops:
  0.6 0.0 copy-start.4
  0.6 0.7 copy-done.4
  1.3 0.0 copy-start
  1.3 1.1 %copy-done = f32[6,32,8,128]{3,2,1,0:T(8,128)S(1)} copy-done((f32[6,32,8,128]{3,2,1,0:T(8,128)S(1)}, f32[6,32,8,128]{3,2,1,0:T(8,128)}, u32[]{:S(2)}) %copy-start) | copy-done | bytes 786456
  2.4 0.0 copy-start.3
  2.4 0.9 copy-done.3
  3.4 0.0 copy-start.5
  3.4 0.7 copy-done.5
  4.0 0.0 copy-start.6
  4.0 0.7 copy-done.6
  4.7 58.9 %shard_map.131 = (f32[6,32,8,128]{3,2,1,0:T(8,128)S(1)}, f32[4,32,512]{2,1,0:T(8,128)S(1)}) custom-call(f32[6,32,8,128]{3,2,1,0:T(8,128)S(1)} %copy-done, s32[32,8,128]{2,1,0:T(8,128)S(1)} %copy-done.3, f32[4]{0:T(128)S(1)} %copy-done.5, f32[4]{0:T(128)S(1)} %copy-done.6, f32[2,12]{1,0:T(2,128)S(1)} %copy-done.4), custom_call_target="tpu_custom_call" | custom-call | tf_op jit(solution)/shard_map/pallas_call | solution.py:392
  63.6 0.0 copy-done.8
  63.6 0.5 fusion.13
  64.2 0.0 copy-start.11
  64.2 0.1 fusion.11
  64.3 0.1 fusion.8
  64.4 0.6 copy-done.11
  64.9 0.4 fusion
  65.4 0.0 copy-done.9
  65.4 0.2 tile.4
  65.6 0.0 copy-start.10
  65.6 0.0 copy-start.1
  65.6 0.0 copy-start.2
  65.7 0.2 tile.10.mask_ref
  65.9 0.4 copy-done.10
  66.3 0.1 copy.14.shift_ref
  66.4 0.2 copy-done.1
  66.6 0.1 copy-done.2
  66.7 0.3 copy-done.7
  67.0 22.8 %shard_map.132 = f32[32,512]{1,0:T(8,128)S(1)} custom-call(bf16[192,192]{1,0:T(8,128)(2,1)S(1)} %bitcast.17, s32[4,2]{1,0:T(4,128)S(1)} %copy.14.shift_ref, bf16[4,192,192]{2,1,0:T(8,128)(2,1)S(1)} %tile.10.mask_ref, f32[4]{0:T(128)S(1)} %copy-done.7, bf16[512,192]{1,0:T(8,128)(2,1)S(1)} %copy-done.2, bf16[192,1024]{1,0:T(8,128)(2,1)S(1)} %copy-done.1), custom_call_target="tpu_custom_call" | custom-call | tf_op jit(solution)/shard_map/pallas_call | solution.py:613
  89.8 0.9 copy.18
  90.7 0.6 copy.19
  (4 shorter events, 0.0 us)
Async XLA Ops:
  0.6 0.7 copy-start.4
  1.3 1.1 %copy-start = (f32[6,32,8,128]{3,2,1,0:T(8,128)S(1)}, f32[6,32,8,128]{3,2,1,0:T(8,128)}, u32[]{:S(2)}) copy-start(f32[6,32,8,128]{3,2,1,0:T(8,128)} %fields_ref.1) | copy-start | bytes 2359300
  2.4 0.9 copy-start.3
  3.4 0.7 copy-start.5
  4.0 0.7 copy-start.6
  4.7 59.0 %copy-start.8 = (f32[512,192,1,1]{0,1,3,2:T(8,128)S(1)}, f32[512,192,1,1]{0,1,3,2:T(8,128)}, u32[]{:S(2)}) copy-start(f32[512,192,1,1]{0,1,3,2:T(8,128)} %constant.20) | copy-start | bytes 1179652
  64.2 0.8 copy-start.11
  64.3 1.1 %copy-start.9 = (s32[4,96,96]{2,1,0:T(8,128)S(1)}, s32[4,96,96]{2,1,0:T(8,128)}, u32[]{:S(2)}) copy-start(s32[4,96,96]{2,1,0:T(8,128)} %param.17) | copy-start | bytes 442372
  65.6 0.7 copy-start.10
  65.6 1.0 %copy-start.1 = (bf16[192,1024]{1,0:T(8,128)(2,1)S(1)}, bf16[192,1024]{1,0:T(8,128)(2,1)}, u32[]{:S(2)}) copy-start(bf16[192,1024]{1,0:T(8,128)(2,1)} %constant.16.clone.g_ref) | copy-start | bytes 1179652
  65.6 1.1 %copy-start.2 = (bf16[512,192]{1,0:T(8,128)(2,1)S(1)}, bf16[512,192]{1,0:T(8,128)(2,1)}, u32[]{:S(2)}) copy-start(bf16[512,192]{1,0:T(8,128)(2,1)} %constant.15.clone.rows_ref) | copy-start | bytes 589828
  66.3 0.7 copy-start.7

commit v4 on v3

--- a/solution.py
+++ b/solution.py
@@ -15,7 +15,7 @@
 ANGULAR = 0.7
 PRECISE = lax.Precision.HIGHEST
 MESH = pl.DeviceIdType.MESH
-GROUP = 8
+GROUP = 16
 
 
 def peer_at(index, tiles_y):
@@ -45,7 +45,6 @@
     material_ref,
     eps_ref,
     loss_ref,
-    wave_ref,
     final_ref,
     phasor_ref,
     e_ref,
@@ -70,6 +69,7 @@
     recv_sem,
     gather_send,
     gather_recv,
+    wave_ref,
 ):
     count = tiles_x * tiles_y
     depth, cells_x, cells_y = fields_ref.shape[1:]
@@ -85,6 +85,10 @@
     last_col = col_id == cells_y - 1
     first_col = col_id == 0
     blank = jnp.zeros(tile, jnp.float32)
+    for turn in range(STEPS):
+        moment = float(np.float32(ANGULAR) * np.float32(turn + 1))
+        wave_ref[0, turn] = math.cos(moment)
+        wave_ref[1, turn] = math.sin(moment)
 
     has_right_x = at_x < tiles_x - 1
     has_left_x = at_x > 0
@@ -247,7 +251,7 @@
 
     def step(turn, unused):
         odd = lax.rem(turn, 2)
-        for slot in range(6):
+        for slot in (0, 1):
             arrived(slot, odd)
         edge = col_e[odd]
 
@@ -280,6 +284,8 @@
             return packed
 
         lax.fori_loop(0, depth // GROUP, magnetic, 0, unroll=True)
+        for slot in (2, 3, 4, 5):
+            arrived(slot, odd)
         beyond_edges(odd)
         for slot in range(6):
             sent(slot, odd)
@@ -322,7 +328,7 @@
 
         @pl.when(turn < STEPS - 1)
         def _():
-            for slot in range(6):
+            for slot in (0, 1, 4, 5, 2, 3):
                 send(slot, 1 - odd)
 
         for component in range(2):
@@ -384,8 +390,6 @@
 def run_march(fields, material_map, material_eps, material_loss, tiles_x, tiles_y):
     depth, cells_x, cells_y = fields.shape[1:]
     count = tiles_x * tiles_y
-    moments = np.float32(ANGULAR) * np.arange(1, STEPS + 1, dtype=np.float32)
-    wave = jnp.asarray(np.stack((np.cos(moments), np.sin(moments))).astype(np.float32))
     vmem = pl.BlockSpec(memory_space=pltpu.VMEM)
     smem = pl.BlockSpec(memory_space=pltpu.SMEM)
     state = (3, depth + 1, cells_x, cells_y)
@@ -395,7 +399,7 @@
             jax.ShapeDtypeStruct(fields.shape, jnp.float32),
             jax.ShapeDtypeStruct((4, cells_x * tiles_x, cells_y * tiles_y), jnp.float32),
         ),
-        in_specs=[vmem, vmem, smem, smem, smem],
+        in_specs=[vmem, vmem, smem, smem],
         out_specs=(vmem, vmem),
         scratch_shapes=[
             pltpu.VMEM(state, jnp.float32),
@@ -420,11 +424,12 @@
             pltpu.SemaphoreType.DMA((8, 2)),
             pltpu.SemaphoreType.DMA((count,)),
             pltpu.SemaphoreType.DMA((count,)),
+            pltpu.SMEM((2, STEPS), jnp.float32),
         ],
         compiler_params=pltpu.CompilerParams(
             collective_id=0, has_side_effects=True, vmem_limit_bytes=40 * 1024 * 1024
         ),
-    )(fields, material_map, material_eps, material_loss, wave)
+    )(fields, material_map, material_eps, material_loss)
 
 
 def picture(
@@ -453,8 +458,7 @@
     count = tiles_x * tiles_y
     me = lax.axis_index("gx") * tiles_y + lax.axis_index("gy")
     sources = mask_ref.shape[0]
-    size_p = mask_ref.shape[1] // 2
-    size_q = mask_ref.shape[2] // 2
+    size_p, size_q = mask_ref.shape[1:]
     pixels = image_ref.shape[1]
     strip = image_ref.shape[0]
     greet(me, count, tiles_y)
@@ -475,7 +479,10 @@
         rolled = jnp.dot(
             rolled.astype(jnp.bfloat16), pick_q, preferred_element_type=jnp.float32
         )
-        masked = (rolled * mask_ref[source].astype(jnp.float32)).astype(jnp.bfloat16)
+        passed = mask_ref[source].astype(jnp.float32)
+        passed = jnp.concatenate((passed, passed), 1)
+        passed = jnp.concatenate((passed, passed), 0)
+        masked = (rolled * passed).astype(jnp.bfloat16)
         spread = jnp.dot(masked, g_ref[...], preferred_element_type=jnp.float32)
         spread = spread.astype(jnp.bfloat16)
         for block in range(2):
@@ -677,11 +684,10 @@
     scaling = 1.0 / math.sqrt(period_x * period_y * STEPS)
     orders_b = (orders * scaling).astype(jnp.bfloat16).reshape(2 * orders_p, 2 * orders_q)
     row_table, g_matrix = image_tables(M, orders_p, orders_q)
-    mask = jnp.tile(source_mask.astype(jnp.bfloat16), (1, 2, 2))
     image = run_picture(
         orders_b,
         source_shift,
-        mask,
+        source_mask,
         source_weight,
         jnp.asarray(row_table),
         jnp.asarray(g_matrix),

time: 91.6 us -> 87.4 us (0.954)
  Pallas kernels: 81.7 us -> 79.1 us
  local copies, waits for them, and re-layouts: 7.69 us -> 6.2 us
    pallas_call x1, Pallas kernels: 58.9 us -> 56.6 us  [run_march(): pl.pallas_call(functools.partial(march, tiles_x, tiles_y), out_shape=(jax...]
    unnamed x27 -> x25, local copies, waits for them, and re-layouts: 7.28 us -> 6.2 us
where the time goes in v4:
time: 87.4 us; the launch traced here: 87.2 us
  Pallas kernels  79.1 us (91%)
  local copies, waits for them, and re-layouts  6.2 us (7%)
  matrix products  0.98 us (1%)
    pallas_call x1, Pallas kernels, run_march(): pl.pallas_call(functools.partial(march, tiles_x, tiles_y), out_shape=(jax...  56.6 us
    pallas_call x1, Pallas kernels, run_picture(): pl.pallas_call(functools.partial(picture, tiles_x, tiles_y), out_shape=ja...  22.5 us
    unnamed x25, local copies, waits for them, and re-layouts  6.2 us

profile of v4, /device:TPU:0, one launch (start us, length us, event | category | flops | bytes accessed | tf_op | source)
XLA Modules:
  0.0 87.2 jit_solution(7001416462941457246)
XLA Ops:
  0.6 0.0 copy-start
  0.6 1.1 %copy-done = f32[6,32,8,128]{3,2,1,0:T(8,128)S(1)} copy-done((f32[6,32,8,128]{3,2,1,0:T(8,128)S(1)}, f32[6,32,8,128]{3,2,1,0:T(8,128)}, u32[]{:S(2)}) %copy-start) | copy-done | bytes 786456
  1.8 0.0 copy-start.4
  1.8 0.9 %copy-done.4 = s32[32,8,128]{2,1,0:T(8,128)S(1)} copy-done((s32[32,8,128]{2,1,0:T(8,128)S(1)}, s32[32,8,128]{2,1,0:T(8,128)}, u32[]{:S(2)}) %copy-start.4) | copy-done | bytes 131096
  2.7 0.0 copy-start.6
  2.7 0.7 copy-done.6
  3.3 0.0 copy-start.7
  3.3 0.7 copy-done.7
  4.0 0.0 copy-start.8
  4.0 56.6 %shard_map.122 = (f32[6,32,8,128]{3,2,1,0:T(8,128)S(1)}, f32[4,32,512]{2,1,0:T(8,128)S(1)}) custom-call(f32[6,32,8,128]{3,2,1,0:T(8,128)S(1)} %copy-done, s32[32,8,128]{2,1,0:T(8,128)S(1)} %copy-done.4, f32[4]{0:T(128)S(1)} %copy-done.6, f32[4]{0:T(128)S(1)} %copy-done.7), custom_call_target="tpu_custom_call" | custom-call | tf_op jit(solution)/shard_map/pallas_call | solution.py:396
  60.6 0.0 copy-done.8
  60.6 0.0 copy-start.10
  60.6 0.0 copy-start.2
  60.6 0.0 copy-start.3
  60.7 0.6 fusion.13
  61.2 0.0 copy-start.1
  61.2 0.1 fusion.11
  61.3 0.1 fusion.8
  61.4 0.0 copy-done.10
  61.4 0.4 fusion
  61.8 0.0 copy-start.9
  61.8 0.7 copy-done.9
  62.5 0.0 copy-start.5
  62.5 0.1 copy.13.shift_ref
  62.6 0.0 copy-done.2
  62.6 0.0 copy-done.3
  62.6 0.0 copy-done.1
  62.6 0.6 copy-done.5
  63.2 22.5 %shard_map.123 = f32[32,512]{1,0:T(8,128)S(1)} custom-call(bf16[192,192]{1,0:T(8,128)(2,1)S(1)} %bitcast.17, s32[4,2]{1,0:T(4,128)S(1)} %copy.13.shift_ref, s32[4,96,96]{2,1,0:T(8,128)S(1)} %copy-done.3, f32[4]{0:T(128)S(1)} %copy-done.5, bf16[512,192]{1,0:T(8,128)(2,1)S(1)} %copy-done.2, bf16[192,1024]{1,0:T(8,128)(2,1)S(1)} %copy-done.1), custom_call_target="tpu_custom_call" | custom-call | tf_op jit(solution)/shard_map/pallas_call | solution.py:620
  85.7 0.9 %copy.17 = f32[6,32,8,128]{3,2,1,0:T(8,128)} copy(f32[6,32,8,128]{3,2,1,0:T(8,128)S(1)} %get-tuple-element.10) | data formatting | bytes 1572864
  86.5 0.6 copy.18
Async XLA Ops:
  0.6 1.1 %copy-start = (f32[6,32,8,128]{3,2,1,0:T(8,128)S(1)}, f32[6,32,8,128]{3,2,1,0:T(8,128)}, u32[]{:S(2)}) copy-start(f32[6,32,8,128]{3,2,1,0:T(8,128)} %fields_ref.1) | copy-start | bytes 2359300
  1.8 0.9 %copy-start.4 = (s32[32,8,128]{2,1,0:T(8,128)S(1)}, s32[32,8,128]{2,1,0:T(8,128)}, u32[]{:S(2)}) copy-start(s32[32,8,128]{2,1,0:T(8,128)} %material_ref.1) | copy-start | bytes 393220
  2.7 0.7 copy-start.6
  3.3 0.7 copy-start.7
  4.0 56.6 %copy-start.8 = (f32[512,192,1,1]{0,1,3,2:T(8,128)S(1)}, f32[512,192,1,1]{0,1,3,2:T(8,128)}, u32[]{:S(2)}) copy-start(f32[512,192,1,1]{0,1,3,2:T(8,128)} %constant.17) | copy-start | bytes 1179652
  60.6 0.8 copy-start.10
  60.6 2.0 %copy-start.2 = (bf16[512,192]{1,0:T(8,128)(2,1)S(1)}, bf16[512,192]{1,0:T(8,128)(2,1)}, u32[]{:S(2)}) copy-start(bf16[512,192]{1,0:T(8,128)(2,1)} %constant.12.clone.rows_ref) | copy-start | bytes 589828
  60.6 2.0 %copy-start.3 = (s32[4,96,96]{2,1,0:T(8,128)S(1)}, s32[4,96,96]{2,1,0:T(8,128)}, u32[]{:S(2)}) copy-start(s32[4,96,96]{2,1,0:T(8,128)} %mask_ref.1) | copy-start | bytes 442372
  61.2 1.4 %copy-start.1 = (bf16[192,1024]{1,0:T(8,128)(2,1)S(1)}, bf16[192,1024]{1,0:T(8,128)(2,1)}, u32[]{:S(2)}) copy-start(bf16[192,1024]{1,0:T(8,128)(2,1)} %constant.13.clone.g_ref) | copy-start | bytes 1179652
  61.8 0.7 copy-start.9
  62.5 0.7 copy-start.5

commit v5 on v4

--- a/solution.py
+++ b/solution.py
@@ -15,7 +15,7 @@
 ANGULAR = 0.7
 PRECISE = lax.Precision.HIGHEST
 MESH = pl.DeviceIdType.MESH
-GROUP = 16
+GROUP = 32
 
 
 def peer_at(index, tiles_y):
@@ -495,7 +495,7 @@
             columns[source, size_p:, at + pixels : at + 2 * pixels] = real
         return unused
 
-    lax.fori_loop(0, sources, prepare, 0)
+    lax.fori_loop(0, sources, prepare, 0, unroll=True)
 
     pairs = tiles_x // 2
     at_x = lax.axis_index("gx")

time: 87.4 us -> 86.3 us (0.987)
  Pallas kernels: 79.1 us -> 78 us
where the time goes in v5:
time: 86.3 us; the launch traced here: 86.1 us
  Pallas kernels  78 us (90%)
  local copies, waits for them, and re-layouts  6.2 us (7%)
  matrix products  0.98 us (1%)
    pallas_call x1, Pallas kernels, run_march(): pl.pallas_call(functools.partial(march, tiles_x, tiles_y), out_shape=(jax...  55.9 us
    pallas_call x1, Pallas kernels, run_picture(): pl.pallas_call(functools.partial(picture, tiles_x, tiles_y), out_shape=ja...  22.1 us
    unnamed x25, local copies, waits for them, and re-layouts  6.2 us

profile of v5, /device:TPU:0, one launch (start us, length us, event | category | flops | bytes accessed | tf_op | source)
XLA Modules:
  0.0 86.1 jit_solution(7261582958251534659)
XLA Ops:
  0.6 0.0 copy-start
  0.6 1.1 %copy-done = f32[6,32,8,128]{3,2,1,0:T(8,128)S(1)} copy-done((f32[6,32,8,128]{3,2,1,0:T(8,128)S(1)}, f32[6,32,8,128]{3,2,1,0:T(8,128)}, u32[]{:S(2)}) %copy-start) | copy-done | bytes 786456
  1.8 0.0 copy-start.4
  1.8 0.9 %copy-done.4 = s32[32,8,128]{2,1,0:T(8,128)S(1)} copy-done((s32[32,8,128]{2,1,0:T(8,128)S(1)}, s32[32,8,128]{2,1,0:T(8,128)}, u32[]{:S(2)}) %copy-start.4) | copy-done | bytes 131096
  2.7 0.0 copy-start.6
  2.7 0.7 copy-done.6
  3.3 0.0 copy-start.7
  3.3 0.7 copy-done.7
  4.0 0.0 copy-start.8
  4.0 55.9 %shard_map.122 = (f32[6,32,8,128]{3,2,1,0:T(8,128)S(1)}, f32[4,32,512]{2,1,0:T(8,128)S(1)}) custom-call(f32[6,32,8,128]{3,2,1,0:T(8,128)S(1)} %copy-done, s32[32,8,128]{2,1,0:T(8,128)S(1)} %copy-done.4, f32[4]{0:T(128)S(1)} %copy-done.6, f32[4]{0:T(128)S(1)} %copy-done.7), custom_call_target="tpu_custom_call" | custom-call | tf_op jit(solution)/shard_map/pallas_call | solution.py:396
  59.9 0.0 copy-done.8
  59.9 0.0 copy-start.10
  59.9 0.0 copy-start.2
  60.0 0.0 copy-start.3
  60.0 0.6 fusion.13
  60.5 0.0 copy-start.1
  60.5 0.1 fusion.11
  60.6 0.1 fusion.8
  60.7 0.0 copy-done.10
  60.7 0.4 fusion
  61.1 0.0 copy-start.9
  61.2 0.7 copy-done.9
  61.8 0.0 copy-start.5
  61.8 0.1 copy.13.shift_ref
  61.9 0.0 copy-done.2
  61.9 0.0 copy-done.3
  61.9 0.0 copy-done.1
  61.9 0.6 copy-done.5
  62.5 22.1 %shard_map.123 = f32[32,512]{1,0:T(8,128)S(1)} custom-call(bf16[192,192]{1,0:T(8,128)(2,1)S(1)} %bitcast.17, s32[4,2]{1,0:T(4,128)S(1)} %copy.13.shift_ref, s32[4,96,96]{2,1,0:T(8,128)S(1)} %copy-done.3, f32[4]{0:T(128)S(1)} %copy-done.5, bf16[512,192]{1,0:T(8,128)(2,1)S(1)} %copy-done.2, bf16[192,1024]{1,0:T(8,128)(2,1)S(1)} %copy-done.1), custom_call_target="tpu_custom_call" | custom-call | tf_op jit(solution)/shard_map/pallas_call | solution.py:620
  84.6 0.9 %copy.17 = f32[6,32,8,128]{3,2,1,0:T(8,128)} copy(f32[6,32,8,128]{3,2,1,0:T(8,128)S(1)} %get-tuple-element.10) | data formatting | bytes 1572864
  85.5 0.6 copy.18
Async XLA Ops:
  0.6 1.1 %copy-start = (f32[6,32,8,128]{3,2,1,0:T(8,128)S(1)}, f32[6,32,8,128]{3,2,1,0:T(8,128)}, u32[]{:S(2)}) copy-start(f32[6,32,8,128]{3,2,1,0:T(8,128)} %fields_ref.1) | copy-start | bytes 2359300
  1.8 0.9 %copy-start.4 = (s32[32,8,128]{2,1,0:T(8,128)S(1)}, s32[32,8,128]{2,1,0:T(8,128)}, u32[]{:S(2)}) copy-start(s32[32,8,128]{2,1,0:T(8,128)} %material_ref.1) | copy-start | bytes 393220
  2.7 0.7 copy-start.6
  3.3 0.7 copy-start.7
  4.0 55.9 %copy-start.8 = (f32[512,192,1,1]{0,1,3,2:T(8,128)S(1)}, f32[512,192,1,1]{0,1,3,2:T(8,128)}, u32[]{:S(2)}) copy-start(f32[512,192,1,1]{0,1,3,2:T(8,128)} %constant.17) | copy-start | bytes 1179652
  59.9 0.8 copy-start.10
  59.9 2.0 %copy-start.2 = (bf16[512,192]{1,0:T(8,128)(2,1)S(1)}, bf16[512,192]{1,0:T(8,128)(2,1)}, u32[]{:S(2)}) copy-start(bf16[512,192]{1,0:T(8,128)(2,1)} %constant.12.clone.rows_ref) | copy-start | bytes 589828
  60.0 2.0 %copy-start.3 = (s32[4,96,96]{2,1,0:T(8,128)S(1)}, s32[4,96,96]{2,1,0:T(8,128)}, u32[]{:S(2)}) copy-start(s32[4,96,96]{2,1,0:T(8,128)} %mask_ref.1) | copy-start | bytes 442372
  60.5 1.4 %copy-start.1 = (bf16[192,1024]{1,0:T(8,128)(2,1)S(1)}, bf16[192,1024]{1,0:T(8,128)(2,1)}, u32[]{:S(2)}) copy-start(bf16[192,1024]{1,0:T(8,128)(2,1)} %constant.13.clone.g_ref) | copy-start | bytes 1179652
  61.1 0.7 copy-start.9
  61.8 0.7 copy-start.5
